TPU v7x, 256 devices: a whole 4x4x8 slice. The times are simulated.
256 devices in a mesh: dp: 8 (over x, core), segment: 2 (over y_hi), blk: 16 (over y_lo, z).
Axes of the slice: x: 4, y: 4 (y_hi: 2, y_lo: 2; y = y_hi * 2 + y_lo), z: 8, core: 2. Of those that a mesh axis runs over, the one named last changes fastest.
Arguments:
- tokens: bfloat16 [8, 6144, 1280], P('dp', 'blk'), may hold values from -6 to 6
- targets: bfloat16 [8, 6144, 1176], P('dp', 'blk'), may hold values from -6 to 6
- visible: int32 [8, 6144], P('dp', 'blk'), may hold values from 0 to 1, as said below
- w_qkv: bfloat16 [1280, 1920], replicated, as said below
- w_out: bfloat16 [640, 1280], replicated, may hold values from -0.25 to 0.25
- w_embed: bfloat16 [1280, 512], replicated, may hold values from -0.15625 to 0.15625
- mask_token: bfloat16 [512], replicated, may hold values from -4 to 4
- dec_pos: bfloat16 [6144, 512], P('blk'), may hold values from -4 to 4
- w_up: bfloat16 [512, 1024], replicated, may hold values from -0.25 to 0.25
- w_down: bfloat16 [1024, 512], replicated, may hold values from -0.1875 to 0.1875
- w_head: bfloat16 [512, 1176], replicated, may hold values from -0.25 to 0.25
Outputs:
- grad_w_out: float32 [640, 1280], P('blk', ('dp', 'segment'))
- grad_w_up: float32 [512, 1024], P('blk', ('dp', 'segment'))
- grad_w_down: float32 [1024, 512], P('blk', ('dp', 'segment'))
Inputs may be any that keep to these rules, and one draw needn't show every extreme that they name: In each scene every tile of 384 consecutive patches has at most 168 visible patches and one tile exactly 168; each scene has 1536 visible patches. `w_qkv`: the query, key and value projections side by side, 640 columns each.
All inputs are finite; a program needn't handle non-finite values.
Results may differ from a plain program's by a relative error of at most 0.018.
Values may be sent and summed in bfloat16 or wider, within the bound.
A program may use at most 128 MiB of HBM per device.

v0:
```python
import math

import jax
import jax.numpy as jnp
from jax import lax
from jax.sharding import PartitionSpec as P

HEADS = 8
HEAD_DIM = 80
VIS_TILE = 96
TILE_CAP = 168


epsilon = 1e-05


def shifted(block, axis, distance):
    devices = range(lax.axis_size(axis))
    route = [(i - distance, i) for i in devices if i - distance in devices]
    return lax.ppermute(block, axis, route)


def layer_norm(matrix):
    center = matrix - jnp.mean(matrix, axis=-1, keepdims=True)
    return center * lax.rsqrt(jnp.mean(center * center, axis=-1, keepdims=True) + epsilon)


def norm_backward(matrix, gradient):
    center = matrix - jnp.mean(matrix, axis=-1, keepdims=True)
    inverse = lax.rsqrt(jnp.mean(center * center, axis=-1, keepdims=True) + epsilon)
    normal_rows = center * inverse
    cross_mean = jnp.mean(gradient * normal_rows, axis=-1, keepdims=True)
    return inverse * (
        gradient - jnp.mean(gradient, axis=-1, keepdims=True) - normal_rows * cross_mean
    )


def gelu_exact(inputs):
    return 0.5 * inputs * (1.0 + lax.erf(inputs * (1.0 / math.sqrt(2.0))))


def gelu_slope(inputs):
    cumulative = 0.5 * (1.0 + lax.erf(inputs * (1.0 / math.sqrt(2.0))))
    return cumulative + inputs * jnp.exp(-0.5 * inputs * inputs) * (1.0 / math.sqrt(2.0 * math.pi))


def slot_table(tile_seen, slot_count):
    position = jnp.cumsum(tile_seen, dtype=jnp.int32) - 1
    slot_ids = jnp.arange(slot_count, dtype=jnp.int32)
    hits = (position[None, :] == slot_ids[:, None]) & (tile_seen[None, :] == 1)
    return (hits.astype(jnp.bfloat16), position)


def attend(query, keys, values, key_valid):
    query_count = query.shape[0]
    key_count = keys.shape[0]
    query_heads = query.reshape(query_count, HEADS, HEAD_DIM)
    key_heads = keys.reshape(key_count, HEADS, HEAD_DIM)
    value_heads = values.reshape(key_count, HEADS, HEAD_DIM)
    scores = jnp.einsum(
        "qhd,khd->hqk", query_heads, key_heads, preferred_element_type=jnp.float32
    ) * (1.0 / math.sqrt(HEAD_DIM))
    scores = jnp.where(key_valid[None, None, :] > 0, scores, -1e30)
    probs = jax.nn.softmax(scores, axis=-1).astype(jnp.bfloat16)
    attended = jnp.einsum("hqk,khd->qhd", probs, value_heads, preferred_element_type=jnp.float32)
    return attended.reshape(query_count, HEADS * HEAD_DIM).astype(jnp.bfloat16)


def decode(
    embedded,
    selector,
    position,
    tile_seen,
    tile_targets,
    mask_token,
    tile_pos,
    w_up,
    w_down,
    w_head,
    grad_scale,
):
    seen_rows = (tile_seen == 1)[:, None]
    spread = jnp.take(embedded, jnp.clip(position, 0, embedded.shape[0] - 1), axis=0)
    stream = jnp.where(
        seen_rows, spread, mask_token.astype(jnp.float32)[None, :]
    ) + tile_pos.astype(jnp.float32)
    unit = layer_norm(stream).astype(jnp.bfloat16)
    hidden_in = jnp.dot(unit, w_up, preferred_element_type=jnp.float32)
    active = gelu_exact(hidden_in).astype(jnp.bfloat16)
    stream_out = stream + jnp.dot(active, w_down, preferred_element_type=jnp.float32)
    predicted = jnp.dot(stream_out.astype(jnp.bfloat16), w_head, preferred_element_type=jnp.float32)
    pred_grad = ((predicted - tile_targets.astype(jnp.float32)) * grad_scale).astype(jnp.bfloat16)
    out_grad = jnp.dot(pred_grad, w_head.T, preferred_element_type=jnp.float32)
    out_grad_low = out_grad.astype(jnp.bfloat16)
    grad_down = jnp.dot(active.T, out_grad_low, preferred_element_type=jnp.float32)
    active_grad = jnp.dot(out_grad_low, w_down.T, preferred_element_type=jnp.float32)
    hidden_grad = (active_grad * gelu_slope(hidden_in)).astype(jnp.bfloat16)
    grad_up = jnp.dot(unit.T, hidden_grad, preferred_element_type=jnp.float32)
    unit_grad = jnp.dot(hidden_grad, w_up.T, preferred_element_type=jnp.float32)
    stream_grad = out_grad + norm_backward(stream, unit_grad)
    row_grad = jnp.where(seen_rows, stream_grad, 0.0).astype(jnp.bfloat16)
    slot_grad = jnp.dot(selector, row_grad, preferred_element_type=jnp.float32).astype(jnp.bfloat16)
    return (slot_grad, grad_up, grad_down)


def on_device(
    tokens, targets, visible, w_qkv, w_out, w_embed, mask_token, dec_pos, w_up, w_down, w_head
):
    tile_rows = tokens[0]
    tile_targets = targets[0]
    tile_seen = visible[0]
    model_width = tile_rows.shape[1]
    inner_width = w_out.shape[0]
    decoder_width = w_embed.shape[1]
    hidden_width = w_up.shape[1]
    selector, position = slot_table(tile_seen, TILE_CAP)
    seen_count = jnp.sum(tile_seen, dtype=jnp.int32)
    slot_valid = (jnp.arange(TILE_CAP, dtype=jnp.int32) < seen_count).astype(jnp.bfloat16)
    encoder_side = lax.axis_index("segment") == 0
    decoder_side = jnp.logical_not(encoder_side)
    masked_all = lax.axis_size("dp") * lax.axis_size("blk") * (tile_rows.shape[0] - VIS_TILE)
    grad_scale = 8.0 / math.sqrt(masked_all)

    def front():
        packed = jnp.dot(selector, tile_rows, preferred_element_type=jnp.float32).astype(
            jnp.bfloat16
        )
        normed = layer_norm(packed.astype(jnp.float32)).astype(jnp.bfloat16)
        projected = jnp.dot(normed, w_qkv, preferred_element_type=jnp.float32).astype(jnp.bfloat16)
        return (packed, projected)

    def front_unused():
        return (
            jnp.zeros((TILE_CAP, model_width), jnp.bfloat16),
            jnp.zeros((TILE_CAP, 3 * inner_width), jnp.bfloat16),
        )

    packed, projected = lax.cond(encoder_side, front, front_unused)
    gathered, gathered_valid = (
        lax.all_gather(projected[:, inner_width:], "blk", axis=0, tiled=True),
        lax.all_gather(slot_valid, "blk", axis=0, tiled=True),
    )

    def encode():
        attended = attend(
            projected[:, :inner_width],
            gathered[:, :inner_width],
            gathered[:, inner_width:],
            gathered_valid,
        )
        encoded = (
            packed.astype(jnp.float32)
            + jnp.dot(attended, w_out, preferred_element_type=jnp.float32)
        ).astype(jnp.bfloat16)
        return (attended, encoded)

    zero_up = jnp.zeros((decoder_width, hidden_width), jnp.float32)
    zero_down = jnp.zeros((hidden_width, decoder_width), jnp.float32)

    def encode_unused():
        return (
            jnp.zeros((TILE_CAP, inner_width), jnp.bfloat16),
            jnp.zeros((TILE_CAP, model_width), jnp.bfloat16),
        )

    attended, encoded = lax.cond(encoder_side, encode, encode_unused)
    arrived = shifted(encoded, "segment", 1)

    def decoder_work():
        embedded = jnp.dot(arrived, w_embed, preferred_element_type=jnp.float32)
        slot_grad, grad_up, grad_down = decode(
            embedded,
            selector,
            position,
            tile_seen,
            tile_targets,
            mask_token,
            dec_pos,
            w_up,
            w_down,
            w_head,
            grad_scale,
        )
        sent_grad = jnp.dot(slot_grad, w_embed.T, preferred_element_type=jnp.float32).astype(
            jnp.bfloat16
        )
        return (sent_grad, grad_up, grad_down)

    def decoder_unused():
        return (jnp.zeros((TILE_CAP, model_width), jnp.bfloat16), zero_up, zero_down)

    sent_grad, grad_up, grad_down = lax.cond(decoder_side, decoder_work, decoder_unused)
    encoded_grad = shifted(sent_grad, "segment", -1)

    def out_term():
        return jnp.dot(attended.T, encoded_grad, preferred_element_type=jnp.float32)

    def out_unused():
        return jnp.zeros((inner_width, model_width), jnp.float32)

    grad_out = lax.cond(encoder_side, out_term, out_unused)
    terms = (grad_out, grad_up, grad_down)
    partial_sums = (
        lax.psum_scatter(
            terms[0].astype(jnp.bfloat16), "blk", scatter_dimension=0, tiled=True
        ).astype(jnp.float32),
        lax.psum_scatter(
            terms[1].astype(jnp.bfloat16), "blk", scatter_dimension=0, tiled=True
        ).astype(jnp.float32),
        lax.psum_scatter(
            terms[2].astype(jnp.bfloat16), "blk", scatter_dimension=0, tiled=True
        ).astype(jnp.float32),
    )
    finished = (
        lax.psum_scatter(partial_sums[0], ("dp", "segment"), scatter_dimension=1, tiled=True),
        lax.psum_scatter(partial_sums[1], ("dp", "segment"), scatter_dimension=1, tiled=True),
        lax.psum_scatter(partial_sums[2], ("dp", "segment"), scatter_dimension=1, tiled=True),
    )
    return (finished[0], finished[1], finished[2])


def solution(mesh):
    in_specs = (
        P("dp", "blk", None),
        P("dp", "blk", None),
        P("dp", "blk"),
        P(),
        P(),
        P(),
        P(),
        P("blk", None),
        P(),
        P(),
        P(),
    )
    out_specs = (
        P("blk", ("dp", "segment")),
        P("blk", ("dp", "segment")),
        P("blk", ("dp", "segment")),
    )
    return jax.shard_map(
        on_device, mesh=mesh, in_specs=in_specs, out_specs=out_specs, check_vma=False
    )
```

profile of v0, /device:TPU:1, one launch (start us, length us, event | category | flops | bytes accessed | tf_op | source)
XLA Modules:
  0.0 625.2 jit_solution(6674640791340104089)
XLA Ops:
  7.2 0.0 all-gather.2.cloned.1.call-start
  7.2 0.7 compare_reduce_fusion.1
  7.9 1.3 fusion.60
  9.2 0.3 reduce-window.9
  9.5 0.1 slice.19
  9.7 0.1 slice_reduce_fusion
  9.8 0.1 add_bitcast_fusion
  9.9 0.1 fusion.58
  9.9 7.3 %conditional.4 = (bf16[168,1280]{1,0:T(8,128)(2,1)}, bf16[168,1920]{1,0:T(8,128)(2,1)S(1)}) conditional(s32[]{:T(128)} %convert_element_type.102, () %tuple.40, (bf16[1,384,1280]{2,1,0:T(8,128)(2,1)}, bf16[168,384]{1,0:T(8,128)(2,1)S(1)}, bf16[1280,1920]{1,0:T(8,128)(2,1)}) %tuple.41), branch_computations={%region_2.3_spmd, %region_3.6_spmd} | conditional | flops 993592512 | bytes 7968688 | solution.py:138
  9.9 2.3 convert_reduce_fusion
  12.3 1.3 fusion.3
  13.6 3.7 convolution_convert_fusion.1
  17.3 0.8 slice.21
  18.0 0.0 all-gather.2.cloned.1.call-update
  18.1 0.0 reduce-scatter.15.cloned.1.call-start
  18.1 0.6 dynamic-slice
  19.4 0.7 compare_convert_fusion
  20.0 0.2 dynamic-update-slice
  20.3 34.6 %all-reduce = bf16[2688]{0:T(1024)(128)(2,1)S(1)} all-reduce(bf16[2688]{0:T(1024)(128)(2,1)S(1)} %dynamic-update-slice), channel_id=1, replica_groups=mesh['dp'=8,'segment'=2,'blk'=16] {'blk'}, use_global_device_ids=true, to_apply=%add | all-reduce | flops 2688 | bytes 10752
  54.8 52.7 %all-gather.2.cloned.1.call-done = bf16[2688,1280]{1,0:T(8,128)(2,1)} async-done(((bf16[168,1280]{1,0:T(8,128)(2,1)}), bf16[2688,1280]{1,0:T(8,128)(2,1)}) %all-gather.2.cloned.1.call-update) | async-done | bytes 6881296 | tf_op jit(solution)/shard_map/all_gather | solution.py:140
  107.5 40.2 %conditional.5 = (bf16[168,640]{0,1:T(8,128)(2,1)}, bf16[168,1280]{1,0:T(8,128)(2,1)S(1)}) conditional(s32[]{:T(128)} %convert_element_type.102, () %tuple.39, (bf16[2688]{0:T(1024)(128)(2,1)S(1)}, bf16[168,1920]{1,0:T(8,128)(2,1)S(1)}, bf16[2688,1280]{1,0:T(8,128)(2,1)}, bf16[168,1280]{1,0:T(8,128)(2,1)}, bf16[640,1280]{1,0:T(8,128)(2,1)}) %tuple.42), branch_computations={%region_7.8_spmd, %region_8.0_spmd} | conditional | flops 1453740288 | bytes 74746920 | solution.py:166
  107.5 0.9 copy.36
  108.5 9.9 %copy.37 = bf16[2688,1280]{0,1:T(8,128)(2,1)} copy(bf16[2688,1280]{1,0:T(8,128)(2,1)} %get-tuple-element.156) | data formatting | bytes 13762560 | tf_op jit(solution)/shard_map
  118.3 6.4 %fusion.62 = (bf16[2688,640]{0,1:T(8,128)(2,1)}, bf16[2688,640]{0,1:T(8,128)(2,1)}) fusion(bf16[2688,1280]{0,1:T(8,128)(2,1)} %copy.37), kind=kLoop, calls=%fused_computation.90 | loop fusion | bytes 13762560 | tf_op jit(solution)/shard_map/cond/branch_1_fun/slice | solution.py:147
  124.7 11.7 %fusion.63 = (f32[8,168]{1,0:T(8,128)S(1)}, f32[8,168,2688]{2,1,0:T(8,128)}) fusion(pred[2688]{0:T(1024)(128)(4,1)S(1)} %broadcast_compare_fusion, bf16[168,8,80]{0,2,1:T(8,128)(2,1)S(1)} %bitcast.66, bf16[2688,8,80]{0,2,1:T(8,128)(2,1)} %bitcast.63), kind=kOutput, calls=%fused_computation.91 | convolution fusion | flops 592480896 | bytes 18114432 | tf_op jit(solution)/shard_map/cond/branch_1_fun/sub | solution.py:64
  136.4 9.7 %fusion.15 = bf16[8,168,80]{1,2,0:T(8,128)(2,1)} fusion(bf16[2688,8,80]{0,2,1:T(8,128)(2,1)} %bitcast.62, f32[8,168,2688]{2,1,0:T(8,128)} %get-tuple-element.184, f32[8,168]{1,0:T(8,128)S(1)} %get-tuple-element.183), kind=kOutput, calls=%fused_computation.25 | convolution fusion | flops 585360384 | bytes 18111744 | tf_op jit(solution)/shard_map/cond/branch_1_fun/hqk,khd->qhd/dot_general | solution.py:65
  146.1 1.6 fusion.14
  147.8 0.7 copy-done.9
  148.5 1.3 collective-permute-start
  149.8 9.3 %collective-permute-done = bf16[168,1280]{1,0:T(8,128)(2,1)S(1)} collective-permute-done((bf16[168,1280]{1,0:T(8,128)(2,1)}, bf16[168,1280]{1,0:T(8,128)(2,1)S(1)}, u32[]{:S(2)}, u32[]{:S(2)}) %collective-permute-start) | collective-permute-done | bytes 430112 | tf_op jit(solution)/shard_map/ppermute | solution.py:20
  159.1 3.0 conditional.6
  159.1 0.8 broadcast.157
  159.9 1.0 broadcast_in_dim.49
  161.0 1.1 broadcast_in_dim.48
  162.1 0.0 reduce-scatter.15.cloned.1.call-update
  162.1 0.0 reduce-scatter.13.cloned.1.call-start
  162.1 1.3 collective-permute-start.1
  163.4 31.5 %collective-permute-done.1 = bf16[168,1280]{1,0:T(8,128)(2,1)S(1)} collective-permute-done((bf16[168,1280]{1,0:T(8,128)(2,1)}, bf16[168,1280]{1,0:T(8,128)(2,1)S(1)}, u32[]{:S(2)}, u32[]{:S(2)}) %collective-permute-start.1) | collective-permute-done | bytes 430112 | tf_op jit(solution)/shard_map/ppermute | solution.py:20
  195.0 1.5 conditional.7
  195.0 1.5 fusion.64
  196.5 1.2 copy-done
  197.7 0.0 reduce-scatter.13.cloned.1.call-update
  197.7 0.0 reduce-scatter.23.cloned.1.call-start
  197.8 1.5 copy.40
  199.3 1.3 copy.47
  200.6 0.0 reduce-scatter.23.cloned.1.call-update
  200.6 0.0 reduce-scatter.21.cloned.1.call-start
  200.7 40.1 %reduce-scatter.15.cloned.1.call-done = bf16[32,1024]{1,0:T(8,128)(2,1)} async-done(((bf16[512,1024]{1,0:T(8,128)(2,1)}), bf16[32,1024]{1,0:T(8,128)(2,1)}) %reduce-scatter.15.cloned.1.call-update) | async-done | bytes 65552 | tf_op jit(solution)/shard_map/reduce_scatter | solution.py:207
  240.8 1.8 copy.45
  242.6 0.0 reduce-scatter.21.cloned.1.call-update
  242.6 0.0 reduce-scatter.19.cloned.1.call-start
  242.7 69.8 %reduce-scatter.13.cloned.1.call-done = bf16[40,1280]{1,0:T(8,128)(2,1)} async-done(((bf16[640,1280]{1,0:T(8,128)(2,1)}), bf16[40,1280]{1,0:T(8,128)(2,1)}) %reduce-scatter.13.cloned.1.call-update) | async-done | bytes 102416 | tf_op jit(solution)/shard_map/reduce_scatter | solution.py:204
  312.4 1.9 copy.43
  314.3 0.0 reduce-scatter.19.cloned.1.call-update
  314.4 0.0 reduce-scatter.17.cloned.1.call-start
  314.4 68.2 %reduce-scatter.23.cloned.1.call-done = bf16[64,512]{1,0:T(8,128)(2,1)} async-done(((bf16[1024,512]{1,0:T(8,128)(2,1)}), bf16[64,512]{1,0:T(8,128)(2,1)}) %reduce-scatter.23.cloned.1.call-update) | async-done | bytes 65552
  382.7 1.0 copy.48
  383.6 0.7 convert_element_type.111
  384.3 0.0 reduce-scatter.17.cloned.1.call-update
  384.4 80.8 %reduce-scatter.21.cloned.1.call-done = f32[64,32]{1,0:T(8,128)} async-done(((f32[1024,32]{1,0:T(8,128)}), f32[64,32]{1,0:T(8,128)}) %reduce-scatter.21.cloned.1.call-update) | async-done | bytes 8208
  465.1 1.4 copy.46
  466.6 74.9 %reduce-scatter.19.cloned.1.call-done = f32[80,40]{1,0:T(8,128)} async-done(((f32[1280,40]{1,0:T(8,128)}), f32[80,40]{1,0:T(8,128)}) %reduce-scatter.19.cloned.1.call-update) | async-done | bytes 12816
  541.5 1.5 copy.44
  542.9 75.4 %reduce-scatter.17.cloned.1.call-done = f32[64,32]{0,1:T(8,128)} async-done(((f32[64,512]{0,1:T(8,128)}), f32[64,32]{0,1:T(8,128)}) %reduce-scatter.17.cloned.1.call-update) | async-done | bytes 8208 | tf_op jit(solution)/shard_map/reduce_scatter | solution.py:217
  (18 shorter events, 0.1 us)
Async XLA Ops:
  7.2 100.3 %all-gather.2.cloned.1.call-start = ((), (), s32[]{:S(2)}) async-start(), calls=%async_computation.6 | async-start | bytes 7311360 | tf_op jit(solution)/shard_map/all_gather | solution.py:140
  9.9 8.2 %copy-start.13 = (u32[256]{0:T(256)S(1)}, u32[256]{0:T(256)}, u32[]{:S(2)}) copy-start(u32[256]{0:T(256)} %constant.96) | copy-start | bytes 3076
  18.1 222.8 %reduce-scatter.15.cloned.1.call-start = ((), (), s32[]{:S(2)}) async-start(), calls=%async_computation.8 | async-start | bytes 1114112 | tf_op jit(solution)/shard_map/reduce_scatter | solution.py:207
  107.5 51.6 %copy-start.1 = (bf16[1280,512]{1,0:T(8,128)(2,1)S(1)}, bf16[1280,512]{1,0:T(8,128)(2,1)}, u32[]{:S(2)}) copy-start(bf16[1280,512]{1,0:T(8,128)(2,1)} %param.24) | copy-start | bytes 3932164
  107.5 51.6 %copy-start.11 = (s32[1,384]{1,0:T(1,128)S(1)}, s32[1,384]{1,0:T(1,128)}, u32[]{:S(2)}) copy-start(s32[1,384]{1,0:T(1,128)} %param.21) | copy-start | bytes 4612
  107.5 51.6 %copy-start.12 = (bf16[512]{0:T(512)(128)(2,1)S(1)}, bf16[512]{0:T(512)(128)(2,1)}, u32[]{:S(2)}) copy-start(bf16[512]{0:T(512)(128)(2,1)} %param.25) | copy-start | bytes 3076
  136.4 9.7 %copy-start.7 = (bf16[640,1280]{1,0:T(8,128)(2,1)S(1)}, bf16[640,1280]{1,0:T(8,128)(2,1)}, u32[]{:S(2)}) copy-start(bf16[640,1280]{1,0:T(8,128)(2,1)} %get-tuple-element.101) | copy-start | bytes 4915204 | tf_op jit(solution)/shard_map/cond
  147.8 0.8 copy-start.9
  148.5 10.6 %collective-permute-start = (bf16[168,1280]{1,0:T(8,128)(2,1)}, bf16[168,1280]{1,0:T(8,128)(2,1)S(1)}, u32[]{:S(2)}, u32[]{:S(2)}) collective-permute-start(bf16[168,1280]{1,0:T(8,128)(2,1)} %copy-done.9), channel_id=1, source_target_pairs={{0,16},{1,17},{2,18},{3,19},{4,20},{5,21},{6,22},{7,23},{8,24},{9,... | collective-permute-start | bytes 1290248 | tf_op jit(solution)/shard_map/ppermute | solution.py:20
  162.1 150.3 %reduce-scatter.13.cloned.1.call-start = ((), (), s32[]{:S(2)}) async-start(), calls=%async_computation.7 | async-start | bytes 1740800 | tf_op jit(solution)/shard_map/reduce_scatter | solution.py:204
  162.1 32.8 %collective-permute-start.1 = (bf16[168,1280]{1,0:T(8,128)(2,1)}, bf16[168,1280]{1,0:T(8,128)(2,1)S(1)}, u32[]{:S(2)}, u32[]{:S(2)}) collective-permute-start(bf16[168,1280]{1,0:T(8,128)(2,1)} %get-tuple-element.93), channel_id=1, source_target_pairs={{16,0},{17,1},{18,2},{19,3},{20,4},{21,5},{22,6},{23,7},{24,8},{25... | collective-permute-start | bytes 1290248 | tf_op jit(solution)/shard_map/ppermute | solution.py:20
  196.5 1.2 copy-start
  197.7 184.9 %reduce-scatter.23.cloned.1.call-start = ((), (), s32[]{:S(2)}) async-start(), calls=%async_computation.12 | async-start | bytes 1114112
  200.6 264.5 %reduce-scatter.21.cloned.1.call-start = ((), (), s32[]{:S(2)}) async-start(), calls=%async_computation.11 | async-start | bytes 557056
  242.6 298.8 %reduce-scatter.19.cloned.1.call-start = ((), (), s32[]{:S(2)}) async-start(), calls=%async_computation.10 | async-start | bytes 696320
  314.4 304.0 %reduce-scatter.17.cloned.1.call-start = ((), (), s32[]{:S(2)}) async-start(), calls=%async_computation.9 | async-start | bytes 278528 | tf_op jit(solution)/shard_map/reduce_scatter | solution.py:217
Sparse Core Ops, SparseCore 0:
  18.2 89.2 all-gather.1
  162.2 78.5 reduce-scatter.14
  243.5 68.8 reduce-scatter.12
  314.8 67.8 reduce-scatter.22
  387.1 77.9 reduce-scatter.20
  469.0 72.4 reduce-scatter.18
  546.6 71.7 reduce-scatter.16
where the time goes:
time: 627 us; the launch traced here: 625 us
  waiting for transfers between devices  503 us (80%)
  blocking collectives  34.6 us (6%)
  local copies, waits for them, and re-layouts  34.3 us (5%)
  matrix products  30.6 us (5%)
  between operations  14.9 us (2%)
    unnamed x10, waiting for transfers between devices  224 us
    reduce_scatter x1, waiting for transfers between devices, on_device(): lax.psum_scatter(partial_sums[2], ('dp', 'segment'), scatter_dimension=1,...  75.4 us
    reduce_scatter x1, waiting for transfers between devices, on_device(): lax.psum_scatter(terms[0].astype(jnp.bfloat16), 'blk', scatter_dimension=...  69.8 us
    all_gather x1, waiting for transfers between devices, on_device(): lax.all_gather(projected[:, inner_width:], 'blk', axis=0, tiled=True)  52.7 us
    ppermute x2, waiting for transfers between devices, shifted(): return lax.ppermute(block, axis, route)  40.8 us
    reduce_scatter x1, waiting for transfers between devices, on_device(): lax.psum_scatter(terms[1].astype(jnp.bfloat16), 'blk', scatter_dimension=...  40.1 us
    unnamed x1, blocking collectives  34.6 us
  transfers between devices with their start and end apart: 9, of which 9 were waited for; matrix products, arithmetic and copies ran while one was open for 2% of the time, Pallas kernels for 0%

commit v1 on v0

v1 whole, which is shorter than its diff:
```python
import math

import jax
import jax.numpy as jnp
from jax import lax
from jax.experimental import pallas as pl
from jax.experimental.pallas import tpu as pltpu
from jax.sharding import PartitionSpec as P

MESH = pl.DeviceIdType.MESH
F32 = jnp.float32
BF16 = jnp.bfloat16

HEADS = 8
HEAD_DIM = 80
VIS_TILE = 96
TILE = 384
CAP = 168
ROWS = 176
D = 1280
DEC = 512
FF = 1024
PIX = 1176
INNER = 640
HALF = 192
SLOTS = 96
SEG_STEP = 80
EPS = 1e-05
OUT_MASK = -1e30


def dot(a, b):
    return lax.dot_general(a, b, (((1,), (0,)), ((), ())), preferred_element_type=F32)


def dot_nt(a, b):
    return lax.dot_general(a, b, (((1,), (1,)), ((), ())), preferred_element_type=F32)


def dot_tn(a, b):
    return lax.dot_general(a, b, (((0,), (0,)), ((), ())), preferred_element_type=F32)


def normalize(rows):
    center = rows - jnp.mean(rows, axis=-1, keepdims=True)
    inverse = lax.rsqrt(jnp.mean(center * center, axis=-1, keepdims=True) + EPS)
    return center * inverse, inverse


def iota(shape, axis):
    return lax.broadcasted_iota(jnp.int32, shape, axis)


names = []


def ident(name):
    if name not in names:
        names.append(name)
    return names.index(name)


N_REMOTE = 96
N_LOCAL = 32


def kernel(
    tokens_h, targets_h, vis_ref, wqkv_h, wout_h, wembed_h, mtok_ref, dpos_h, wup_h, wdown_h, whead_h,
    go_ref, gu_ref, gd_ref,
    tokens, targets, wqkv, wout, wembed, dpos, wup, wdown, whead, wperm,
    selector, seen_col, packed, heads, other, kv_own, kv_r, kv_l, kv_d, keys, vals, qx, acc, top,
    att_out, att_in, att, att_sib, pos_slot, tgt_slot, mask_slot,
    unit_m, act_m, og_m, hg_m, unit_ms, act_ms, og_ms, hg_ms, gd_acc, gu_acc,
    unit_v, act_v, og_v, hg_v, sg_v, unit_vs, act_vs, og_vs, hg_vs, sg_vs,
    rs_gd, rs_gu, rs_p, rs_q, rs_x2, rs_y2,
    in_gd, in_gu, in_p, in_q, in_x2, in_y2,
    turned, zs, zr,
    send_sem, recv_sem, load_sem,
):
    dp = lax.axis_index("dp")
    seg = lax.axis_index("segment")
    blk = lax.axis_index("blk")
    x, core = dp // 2, dp % 2
    y, z = seg * 2 + blk // 8, blk % 8
    y_lo = blk // 8

    def device(px, pc, py, pz):
        return (px * 2 + pc, py // 2, (py % 2) * 8 + pz)

    def at_x(step):
        return device((x + step + 4) % 4, core, y, z)

    def at_y(step):
        return device(x, core, (y + step + 4) % 4, z)

    def at_z(step):
        return device(x, core, y, (z + step + 8) % 8)

    sibling = device(x, 1 - core, y, z)

    loads = {}

    def load(name, src, dst):
        copy = pltpu.make_async_copy(src, dst, load_sem.at[len(loads)])
        copy.start()
        loads[name] = copy

    load("tokens", tokens_h, tokens)
    load("wqkv", wqkv_h, wqkv)
    load("dpos", dpos_h, dpos)
    load("targets", targets_h, targets)
    load("wup", wup_h, wup)
    load("wdown", wdown_h, wdown)
    load("whead", whead_h, whead)
    load("wout", wout_h, wout)
    load("wembed", wembed_h, wembed)
    for px in range(4):
        for ps in range(2):
            first = pl.multiple_of((px * 4 + core * 2 + ps) * 80, 16)
            load(
                "wp%d%d" % (px, ps),
                wembed_h.at[pl.ds(first, 48)],
                wperm.at[pl.ds(px * 96 + ps * 48, 48)],
            )
            load(
                "wq%d%d" % (px, ps),
                wembed_h.at[pl.ds(pl.multiple_of(first + 48, 16), 32)],
                wperm.at[pl.ds(384 + ps * 128 + px * 32, 32)],
            )

    barrier = pltpu.get_barrier_semaphore()
    peers = [sibling, at_x(1), at_x(-1), at_y(1), at_y(-1), at_y(2)]
    peers += [at_z(step) for step in range(1, 8)]
    for peer in peers:
        pl.semaphore_signal(barrier, inc=1, device_id=peer, device_id_type=MESH)

    started = []

    def send(name, src, dst, target):
        i = ident(name)
        copy = pltpu.make_async_remote_copy(
            src_ref=src,
            dst_ref=dst,
            send_sem=send_sem.at[i],
            recv_sem=recv_sem.at[i],
            device_id=target,
            device_id_type=MESH,
        )
        copy.start()
        started.append(copy)
        return copy

    vis = vis_ref[...].astype(F32)
    tri = (iota((TILE, TILE), 0) <= iota((TILE, TILE), 1)).astype(F32).astype(BF16)
    vis8 = jnp.broadcast_to(vis, (8, TILE))
    position = dot(vis8.astype(BF16), tri)[0:1, :] - 1.0
    count = jnp.sum(vis, axis=1, keepdims=True)
    slot_ids = iota((ROWS, TILE), 0).astype(F32)
    chosen = jnp.where((position == slot_ids) & (vis > 0.5), 1.0, 0.0).astype(BF16)
    selector[...] = chosen
    loads["tokens"].wait()
    rows = dot(chosen, tokens[...])
    packed[...] = rows.astype(BF16)
    normed = normalize(rows)[0].astype(BF16)
    seen_col[...] = dot_tn(chosen, jnp.ones((ROWS, 128), BF16))
    loads["wqkv"].wait()
    projected = dot(normed, wqkv[...])
    slot_row = iota((ROWS, 256), 0)
    for h in range(HEADS):
        parts = [projected[:, o + h * 80 : o + h * 80 + 80] for o in (640, 1280, 0)]
        block = jnp.concatenate(parts + [jnp.zeros((ROWS, 16), F32)], axis=1)
        block = jnp.where(slot_row >= CAP, count, block)
        heads[h] = block.astype(BF16)

    pl.semaphore_wait(barrier, len(peers))
    up_head = ((y + 1) % 4) * 2
    down_head = ((y + 3) % 4) * 2 + 1
    from_down = send("qkv+", heads.at[up_head], other.at[0], at_y(1))
    from_up = send("qkv-", heads.at[down_head], other.at[1], at_y(-1))

    lane = iota((ROWS, 128), 1)
    slot128 = iota((ROWS, 128), 0).astype(F32)

    def make_query(block, j, first):
        window = pltpu.roll(block[:, 128:256].astype(F32), 96, 1)
        query = jnp.where(lane < 80, window, jnp.where(lane == 80, 1.0, 0.0))
        qx[j, first : first + ROWS, :] = query.astype(BF16)

    def pick_kv(block):
        return block[:, 0:160].astype(F32)

    own = [heads[y * 2], heads[y * 2 + 1]]
    from_down.wait_recv()
    from_up.wait_recv()
    others = [other[0], other[1]]
    kv = [pick_kv(b) for b in own + others]
    kv_own[...] = jnp.concatenate(kv, axis=1).astype(BF16)

    cut = ((0, 96), (96, 80))

    def ring_send(name, src, dst, part, target):
        first, length = cut[part]
        return send(
            name + str(part), src.at[pl.ds(first, length)], dst.at[pl.ds(first, length)], target
        )

    ring = {}
    for part in range(2):
        ring["r0", part] = ring_send("r0", kv_own, kv_r.at[0], part, at_z(1))
        ring["l0", part] = ring_send("l0", kv_own, kv_l.at[0], part, at_z(-1))

    def ring_step(step):
        for part in range(2):
            ring["r%d" % (step - 1), part].wait_recv()
            if step < 3:
                ring["r%d" % step, part] = ring_send(
                    "r%d" % step, kv_r.at[step - 1], kv_r.at[step], part, at_z(1)
                )
            elif part == 0:
                ring["d", 0] = ring_send("d", kv_r.at[2], kv_d, 0, at_z(1))
            ring["l%d" % (step - 1), part].wait_recv()
            if step < 3:
                ring["l%d" % step, part] = ring_send(
                    "l%d" % step, kv_l.at[step - 1], kv_l.at[step], part, at_z(-1)
                )
            elif part == 1:
                ring["d", 1] = ring_send("d", kv_l.at[2], kv_d, 1, at_z(-1))

    def unpack(block, first):
        for i in range(2):
            for j in range(2):
                base = 320 * i + 160 * j
                low = base // 128 * 128
                window = block[:, low : low + 256].astype(F32)
                off = base % 128
                key = window if off == 0 else pltpu.roll(window, 256 - off, 1)
                key = key[:, 0:128]
                value = pltpu.roll(window, 256 - off - 80, 1)[:, 0:128]
                counts = key[CAP : CAP + 1, :]
                outside = jnp.where((lane == 80) & (slot128 >= counts), OUT_MASK, 0.0)
                at = first + i * ROWS
                keys[j, at : at + ROWS, :] = jnp.where(lane < 80, key, outside).astype(BF16)
                vals[j, at : at + ROWS, :] = jnp.where(lane == 80, 1.0, value).astype(BF16)

    scale = math.log2(math.e) / math.sqrt(HEAD_DIM)

    def attend(first, length, begin=False):
        for j in range(2):
            scores = dot_nt(qx[j], keys[j, first : first + length, :])
            best = jnp.max(scores, axis=1, keepdims=True)
            if not begin:
                before = top[j]
                best = jnp.maximum(before[:, 0:1], best)
            probs = jnp.exp2((scores - best) * scale).astype(BF16)
            term = dot(probs, vals[j, first : first + length, :])
            if not begin:
                term = term + acc[j] * jnp.exp2((before - best) * scale)
            acc[j] = term
            top[j] = jnp.broadcast_to(best, (2 * ROWS, 128))

    grad_scale = 8.0 / math.sqrt(8 * 16 * (TILE - VIS_TILE))
    root_half = 1.0 / math.sqrt(2.0)
    order = iota((DEC, DEC), 1)
    source = (order // 32 % 4) * 128 + (order // 256) * 64 + (order // 128 % 2) * 32 + order % 32
    shuffle = (iota((DEC, DEC), 0) == source).astype(F32).astype(BF16)

    def decode_forward(stream, goal, keep, unit, act):
        normal, inverse = normalize(stream)
        low = normal.astype(BF16)
        unit[...] = low
        hidden = dot(low, wup[...])
        cumulative = 0.5 * (1.0 + lax.erf(hidden * root_half))
        active = (hidden * cumulative).astype(BF16)
        act[...] = active
        slope = cumulative + hidden * jnp.exp(-0.5 * hidden * hidden) * (
            1.0 / math.sqrt(2.0 * math.pi)
        )
        stream_out = stream + dot(active, wdown[...])
        predicted = dot(stream_out.astype(BF16), whead[...])
        pred_grad = ((predicted - goal) * (keep * grad_scale)).astype(BF16)
        out_grad = dot_nt(pred_grad, whead[...])
        return normal, inverse, slope, out_grad

    def decode_hidden(out_low, slope, hg):
        hidden_grad = (dot_nt(out_low, wdown[...]) * slope).astype(BF16)
        for c in range(2):
            for px in range(4):
                at = px * 256 + c * 128
                hg[c, :, px * 128 : px * 128 + 128] = hidden_grad[:, at : at + 128]
        return hidden_grad

    def split_out(out_low, og):
        mixed = dot(out_low, shuffle).astype(BF16)
        og[0] = mixed[:, 0:256]
        og[1] = mixed[:, 256:512]

    for j in range(2):
        make_query(own[j], j, 0)
        make_query(others[j], j, ROWS)
    unpack(kv_own, 0)
    attend(0, 2 * ROWS, begin=True)
    for name in ("dpos", "targets", "wup", "wdown", "whead"):
        loads[name].wait()
    ring_step(1)

    part_rows = pl.ds(pl.multiple_of(seg * HALF, 16), HALF)
    stream_m = mtok_ref[...].astype(F32) + dpos[part_rows, :].astype(F32)
    goal_m = targets[part_rows, :].astype(F32)
    keep_m = 1.0 - seen_col[part_rows, :][:, 0:1]
    normal, inverse, slope, out_grad = decode_forward(stream_m, goal_m, keep_m, unit_m, act_m)
    out_low = out_grad.astype(BF16)
    split_out(out_low, og_m)
    decode_hidden(out_low, slope, hg_m)
    masked = [
        send("unit_m", unit_m, unit_ms, sibling),
        send("act_m", act_m, act_ms, sibling),
        send("og_m", og_m.at[1 - core], og_ms, sibling),
        send("hg_m", hg_m.at[1 - core], hg_ms, sibling),
    ]
    unpack(kv_r.at[0], 2 * ROWS)
    unpack(kv_l.at[0], 4 * ROWS)
    attend(2 * ROWS, 4 * ROWS)
    ring_step(2)

    slot_first = pl.multiple_of(seg * SEG_STEP, 16)
    slot_rows = pl.ds(slot_first, SLOTS)
    chosen_part = selector[slot_rows, :]
    pos_slot[...] = dot(chosen_part, dpos[...])
    tgt_slot[...] = dot(chosen_part, targets[...])
    number = iota((SLOTS, 128), 0) + seg * SEG_STEP
    kept = (number.astype(F32) < count) & (number >= seg * SLOTS)
    mask_slot[...] = jnp.where(kept, 1.0, 0.0)

    for copy in masked:
        copy.wait_recv()
    gd_acc[...] = dot_tn(og_m[core], act_m[...]) + dot_tn(og_ms[...], act_ms[...])
    gu_acc[...] = dot_tn(unit_m[...], hg_m[core]) + dot_tn(unit_ms[...], hg_ms[...])
    unpack(kv_r.at[1], 6 * ROWS)
    unpack(kv_l.at[1], 8 * ROWS)
    attend(6 * ROWS, 4 * ROWS)
    ring_step(3)
    unpack(kv_r.at[2], 10 * ROWS)
    unpack(kv_l.at[2], 12 * ROWS)
    attend(10 * ROWS, 4 * ROWS)
    for name in loads:
        if name not in ("tokens", "wqkv", "dpos", "targets", "wup", "wdown", "whead"):
            loads[name].wait()
    ring["d", 0].wait_recv()
    ring["d", 1].wait_recv()
    unpack(kv_d, 14 * ROWS)
    attend(14 * ROWS, 2 * ROWS)

    done = []
    for j in range(2):
        total = acc[j]
        done.append((total * (1.0 / total[:, 80:81]))[:, 0:80])
    both = jnp.concatenate(done + [jnp.zeros((2 * ROWS, 96), F32)], axis=1).astype(BF16)
    att_out[0] = both[0:ROWS]
    att_out[1] = both[ROWS : 2 * ROWS]
    back = []
    for step, i in ((2, 0), (1, 1), (-1, 1)):
        goal_seg = ((y + step + 4) % 4) // 2
        span = pl.ds(pl.multiple_of(goal_seg * SEG_STEP, 16), SLOTS)
        back.append(send("att%d" % (step + 4), att_out.at[i, span], att_in.at[y], at_y(step)))
    att_in[y] = att_out[0, slot_rows, :]
    for copy in back:
        copy.wait_recv()
    attended = jnp.concatenate([att_in[i][:, 0:160].astype(F32) for i in range(4)], axis=1)
    attended = attended.astype(BF16)
    att[...] = attended
    swap_att = send("att_s", att, att_sib, sibling)

    encoded = packed[slot_rows, :].astype(F32) + dot(attended, wout[...])
    embedded = dot(encoded.astype(BF16), wembed[...])
    stream_v = embedded + pos_slot[...]
    normal, inverse, slope, out_grad = decode_forward(
        stream_v, tgt_slot[...], mask_slot[:, 0:1], unit_v, act_v
    )
    swap_unit = send("unit_v", unit_v, unit_vs, sibling)
    swap_act = send("act_v", act_v, act_vs, sibling)
    out_low = out_grad.astype(BF16)
    split_out(out_low, og_v)
    swap_og = send("og_v", og_v.at[1 - core], og_vs, sibling)
    hidden_grad = decode_hidden(out_low, slope, hg_v)
    swap_hg = send("hg_v", hg_v.at[1 - core], hg_vs, sibling)
    unit_grad = dot_nt(hidden_grad, wup[...])
    cross = jnp.mean(unit_grad * normal, axis=-1, keepdims=True)
    middle = jnp.mean(unit_grad, axis=-1, keepdims=True)
    stream_grad = out_grad + inverse * (unit_grad - middle - normal * cross)
    sg_v[...] = stream_grad.astype(BF16)
    swap_sg = send("sg_v", sg_v, sg_vs, sibling)

    def ring_sum(name, chunks, landing, h0, h1, place, at):
        right, left, far = (place + 1) % 4, (place + 3) % 4, (place + 2) % 4
        s0, s1 = pl.ds(0, h0), pl.ds(h0, h1)
        rel0 = send(name + "rel0", chunks.at[far, s0], landing.at[0, s0], at(1))
        rel1 = send(name + "rel1", chunks.at[far, s1], landing.at[0, s1], at(-1))
        dir1 = send(name + "dir1", chunks.at[right, s1], landing.at[1, s1], at(1))
        dir0 = send(name + "dir0", chunks.at[left, s0], landing.at[1, s0], at(-1))
        state = {}

        def relay():
            rel0.wait_recv()
            landing[3, s0, :] = (
                landing[0, s0, :].astype(F32) + chunks[right, s0, :].astype(F32)
            ).astype(BF16)
            state["c0"] = send(name + "c0", landing.at[3, s0], landing.at[2, s0], at(1))
            rel1.wait_recv()
            landing[3, s1, :] = (
                landing[0, s1, :].astype(F32) + chunks[left, s1, :].astype(F32)
            ).astype(BF16)
            state["c1"] = send(name + "c1", landing.at[3, s1], landing.at[2, s1], at(-1))

        def finish():
            dir0.wait_recv()
            dir1.wait_recv()
            state["c0"].wait_recv()
            state["c1"].wait_recv()
            return (
                chunks[place].astype(F32) + landing[1].astype(F32) + landing[2].astype(F32)
            )

        return relay, finish

    swap_act.wait_recv()
    swap_og.wait_recv()
    gd_t = gd_acc[...] + dot_tn(og_v[core], act_v[...]) + dot_tn(og_vs[...], act_vs[...])
    gd_t = gd_t.astype(BF16)
    for py in range(4):
        for px in range(4):
            for k in range(4):
                r = (py // 2) * 128 + px * 32
                c = (py % 2) * 512 + k * 128
                at = px * 128 + k * 32
                rs_gd[py, at : at + 32, :] = gd_t[r : r + 32, c : c + 128]
    relay_gd, finish_gd = ring_sum("gd", rs_gd, in_gd, 256, 256, y, at_y)

    swap_unit.wait_recv()
    swap_hg.wait_recv()
    gu_t = gu_acc[...] + dot_tn(unit_v[...], hg_v[core]) + dot_tn(unit_vs[...], hg_vs[...])
    gu_t = gu_t.astype(BF16)
    for px in range(4):
        rs_gu[px] = gu_t[:, px * 128 : px * 128 + 128]
    relay_gu, finish_gu = ring_sum("gu", rs_gu, in_gu, 256, 256, x, at_x)

    swap_att.wait_recv()
    swap_sg.wait_recv()
    eg = dot_nt(sg_v[...], wperm[...]).astype(BF16)
    eg_s = dot_nt(sg_vs[...], wperm[...]).astype(BF16)
    go_t = (dot_tn(eg, att[...]) + dot_tn(eg_s, att_sib[...])).astype(BF16)
    for px in range(4):
        for k in range(5):
            rs_p[px, 96 * k : 96 * k + 96, :] = go_t[px * 96 : px * 96 + 96, k * 128 : k * 128 + 128]
    relay_p, finish_p = ring_sum("p", rs_p, in_p, 240, 240, x, at_x)
    for py in range(4):
        for px in range(4):
            for k in range(3):
                r = 384 + (py // 2) * 128 + px * 32
                c = ((py % 2) * 2 + k) * 128
                at = px * 96 + k * 32
                rs_q[py, at : at + 32, :] = go_t[r : r + 32, c : c + 128]
    relay_q, finish_q = ring_sum("q", rs_q, in_q, 192, 192, y, at_y)

    relay_gd()
    relay_gu()
    relay_p()
    relay_q()

    gd_1 = finish_gd()
    q_1 = finish_q()
    for px in range(4):
        rs_y2[px, 0:128, :] = gd_1[px * 128 : px * 128 + 128].astype(BF16)
        rs_y2[px, 128:224, :] = q_1[px * 96 : px * 96 + 96].astype(BF16)
    relay_y2, finish_y2 = ring_sum("y2", rs_y2, in_y2, 112, 112, x, at_x)
    gu_1 = finish_gu()
    p_1 = finish_p()
    lane128 = iota((128, 128), 1)
    for py in range(4):
        first = gu_1[(py % 2) * 256 : (py % 2) * 256 + 128]
        second = gu_1[(py % 2) * 256 + 128 : (py % 2) * 256 + 256]
        if py // 2 == 0:
            pair = jnp.where(lane128 < 64, first, pltpu.roll(second, 64, 1))
        else:
            pair = jnp.where(lane128 < 64, pltpu.roll(first, 64, 1), second)
        rs_x2[py, 0:128, :] = pair.astype(BF16)
        for k in range(3):
            r = 96 * ((py % 2) * 2 + k) + (py // 2) * 48
            rs_x2[py, 128 + 48 * k : 176 + 48 * k, :] = p_1[r : r + 48].astype(BF16)
    relay_x2, finish_x2 = ring_sum("x2", rs_x2, in_x2, 144, 128, y, at_y)
    relay_y2()
    relay_x2()
    y_2 = finish_y2()
    x_2 = finish_x2()

    p_rows = jnp.concatenate([x_2[128 + 48 * k : 176 + 48 * k] for k in range(3)], axis=1)
    q_rows = jnp.concatenate([y_2[128 + 32 * k : 160 + 32 * k] for k in range(3)], axis=1)
    go_rows = jnp.concatenate([p_rows, q_rows, jnp.zeros((48, 384), F32)], axis=0)
    turned[0:384, :] = go_rows.T
    turned[384:400, :] = jnp.zeros((16, 128), F32)
    lane32 = iota((32, 128), 1)
    for pz in range(8):
        up = x_2[(pz % 4) * 32 : (pz % 4) * 32 + 32]
        if pz // 4 == 1:
            up = pltpu.roll(up, 64, 1)
        down = y_2[(pz // 2) * 32 : (pz // 2) * 32 + 32]
        if pz % 2 == 0:
            down = pltpu.roll(down, 64, 1)
        zs[pz, 0:32, :] = jnp.where(lane32 < 64, up, down).astype(BF16)
        at = pl.multiple_of(y_lo * 64 + pz * 40, 8)
        zs[pz, 32:80, :] = turned[pl.ds(at, 48), :].astype(BF16)
    last = []
    for step in range(1, 8):
        last.append(send("z%d" % step, zs.at[(z + step) % 8], zr.at[step - 1], at_z(step)))
    result = zs[z].astype(F32)
    for step in range(1, 8):
        last[step - 1].wait_recv()
        result = result + zr[step - 1].astype(F32)
    go_ref[...] = result[32:72, 0:80]
    gu_ref[...] = result[0:32, 0:64]
    gd_ref[...] = result[0:32, :].T[64:128, :]

    for copy in started:
        copy.wait_send()


def on_device(
    tokens, targets, visible, w_qkv, w_out, w_embed, mask_token, dec_pos, w_up, w_down, w_head
):
    names.clear()
    anywhere = pl.BlockSpec(memory_space=pl.ANY)
    vmem = pl.BlockSpec(memory_space=pltpu.VMEM)

    def low(*shape):
        return pltpu.VMEM(shape, BF16)

    def wide(*shape):
        return pltpu.VMEM(shape, F32)

    scratch = [
        low(TILE, D), low(TILE, PIX), low(D, 3 * INNER), low(INNER, D), low(D, DEC),
        low(TILE, DEC), low(DEC, FF), low(FF, DEC), low(DEC, PIX), low(INNER, DEC),
        low(ROWS, TILE), wide(TILE, 128), low(ROWS, D), low(HEADS, ROWS, 256), low(2, ROWS, 256),
        low(ROWS, INNER), low(3, ROWS, INNER), low(3, ROWS, INNER), low(ROWS, INNER),
        low(2, 16 * ROWS, 128), low(2, 16 * ROWS, 128), low(2, 2 * ROWS, 128),
        wide(2, 2 * ROWS, 128), wide(2, 2 * ROWS, 128),
        low(2, ROWS, 256), low(4, SLOTS, 256), low(SLOTS, INNER), low(SLOTS, INNER),
        wide(SLOTS, DEC), wide(SLOTS, PIX), wide(SLOTS, 128),
        low(HALF, DEC), low(HALF, FF), low(2, HALF, 256), low(2, HALF, DEC),
        low(HALF, DEC), low(HALF, FF), low(HALF, 256), low(HALF, DEC),
        wide(256, FF), wide(DEC, DEC),
        low(SLOTS, DEC), low(SLOTS, FF), low(2, SLOTS, 256), low(2, SLOTS, DEC), low(SLOTS, DEC),
        low(SLOTS, DEC), low(SLOTS, FF), low(SLOTS, 256), low(SLOTS, DEC), low(SLOTS, DEC),
        low(4, 512, 128), low(4, 512, 128), low(4, 480, 128), low(4, 384, 128),
        low(4, 272, 128), low(4, 224, 128),
        low(4, 512, 128), low(4, 512, 128), low(4, 480, 128), low(4, 384, 128),
        low(4, 272, 128), low(4, 224, 128),
        wide(400, 128), low(8, 80, 128), low(7, 80, 128),
        pltpu.SemaphoreType.DMA((N_REMOTE,)),
        pltpu.SemaphoreType.DMA((N_REMOTE,)),
        pltpu.SemaphoreType.DMA((N_LOCAL,)),
    ]
    return pl.pallas_call(
        kernel,
        out_shape=(
            jax.ShapeDtypeStruct((40, 80), F32),
            jax.ShapeDtypeStruct((32, 64), F32),
            jax.ShapeDtypeStruct((64, 32), F32),
        ),
        in_specs=[
            anywhere, anywhere, vmem, anywhere, anywhere, anywhere, vmem, anywhere, anywhere,
            anywhere, anywhere,
        ],
        out_specs=(vmem, vmem, vmem),
        scratch_shapes=scratch,
        compiler_params=pltpu.CompilerParams(
            collective_id=0, has_side_effects=True, vmem_limit_bytes=56 * 1024 * 1024
        ),
    )(
        tokens[0], targets[0], visible, w_qkv, w_out, w_embed, mask_token[None, :], dec_pos, w_up,
        w_down, w_head,
    )


def solution(mesh):
    in_specs = (
        P("dp", "blk", None),
        P("dp", "blk", None),
        P("dp", "blk"),
        P(),
        P(),
        P(),
        P(),
        P("blk", None),
        P(),
        P(),
        P(),
    )
    out_specs = (
        P("blk", ("dp", "segment")),
        P("blk", ("dp", "segment")),
        P("blk", ("dp", "segment")),
    )
    return jax.shard_map(
        on_device, mesh=mesh, in_specs=in_specs, out_specs=out_specs, check_vma=False
    )
```

time: 627 us -> 82.4 us (0.13)
  the two profiles are of different devices: /device:TPU:1 before, /device:TPU:8 now
where the time goes in v1:
time: 82.4 us; the launch traced here: 82.1 us
  Pallas kernels  72.3 us (88%)
  local copies, waits for them, and re-layouts  9.18 us (11%)
    pallas_call x1, Pallas kernels, on_device(): pl.pallas_call(kernel, out_shape=(jax.ShapeDtypeStruct((40, 80), F32), ja...  72.3 us
    unnamed x6, local copies, waits for them, and re-layouts  6.38 us

profile of v1, /device:TPU:8, one launch (start us, length us, event | category | flops | bytes accessed | tf_op | source)
XLA Modules:
  0.0 82.1 jit_solution(16012294691065095970)
XLA Ops:
  0.6 0.0 copy-start
  0.6 1.4 %broadcast_in_dim.3.mtok_ref = bf16[1,512]{1,0:T(2,128)(2,1)} reshape(bf16[512]{0:T(512)(128)(2,1)} %param.17) | data formatting | bytes 2048 | tf_op jit(solution)/shard_map/broadcast_in_dim | solution.py:579
  2.0 2.3 %copy.14 = bf16[1,384,1176]{2,1,0:T(8,128)(2,1)} copy(bf16[1,384,1176]{1,2,0:T(8,128)(2,1)} %param.12) | data formatting | bytes 1806336 | tf_op args[1]
  4.3 0.0 copy-done
  4.3 1.4 %copy.15.whead_h = bf16[512,1176]{1,0:T(8,128)(2,1)} copy(bf16[512,1176]{0,1:T(8,128)(2,1)S(1)} %copy-done) | data formatting | bytes 2408448 | tf_op args[10]
  5.7 72.3 %shard_map.130 = (f32[40,80]{1,0:T(8,128)}, f32[32,64]{1,0:T(8,128)}, f32[64,32]{1,0:T(8,128)}) custom-call(bf16[384,1280]{1,0:T(8,128)(2,1)} %bitcast.3, bf16[384,1176]{1,0:T(8,128)(2,1)} %bitcast.2, s32[1,384]{1,0:T(1,128)} %vis_ref.1, bf16[1280,1920]{1,0:T(8,128)(2,1)} %wqkv_h.1, bf16[640,1280]{1,0:T(8,128)(2,1)} %wout_h.1, bf16[1280,512]{1,0:T(8,128)(2,1)} %wembed_h.1, ...), custom_call_target="tpu_custom_call" | custom-call | tf_op jit(solution)/shard_map/pallas_call | solution.py:562
  78.0 1.4 %copy.16 = f32[64,32]{0,1:T(8,128)} copy(f32[64,32]{1,0:T(8,128)} %get-tuple-element.5) | data formatting | bytes 16384 | tf_op jit(solution)/shard_map/pallas_call | solution.py:562
  79.5 1.3 %copy.19 = f32[40,80]{1,0:T(8,128)} copy(f32[40,80]{1,0:T(8,128)} %get-tuple-element.9) | data formatting | bytes 25600
  80.8 1.3 %copy.20 = f32[32,64]{1,0:T(8,128)} copy(f32[32,64]{1,0:T(8,128)} %get-tuple-element.10) | data formatting | bytes 16384
Async XLA Ops:
  0.6 3.6 %copy-start = (bf16[512,1176]{0,1:T(8,128)(2,1)S(1)}, bf16[512,1176]{0,1:T(8,128)(2,1)}, u32[]{:S(2)}) copy-start(bf16[512,1176]{0,1:T(8,128)(2,1)} %param.21) | copy-start | bytes 3612676

commit v2 on v1

v2 whole, which is shorter than its diff:
```python
import math

import jax
import jax.numpy as jnp
from jax import lax
from jax.experimental import pallas as pl
from jax.experimental.pallas import tpu as pltpu
from jax.sharding import PartitionSpec as P

MESH = pl.DeviceIdType.MESH
F32 = jnp.float32
BF16 = jnp.bfloat16

HEADS = 8
HEAD_DIM = 80
VIS_TILE = 96
TILE = 384
CAP = 168
ROWS = 176
D = 1280
DEC = 512
FF = 1024
PIX = 1176
INNER = 640
HALF = 192
SLOTS = 96
SEG_STEP = 80
PART = 448
EPS = 1e-05
OUT_MASK = -1e30


def dot(a, b):
    return lax.dot_general(a, b, (((1,), (0,)), ((), ())), preferred_element_type=F32)


def dot_nt(a, b):
    return lax.dot_general(a, b, (((1,), (1,)), ((), ())), preferred_element_type=F32)


def dot_tn(a, b):
    return lax.dot_general(a, b, (((0,), (0,)), ((), ())), preferred_element_type=F32)


def normalize(rows):
    center = rows - jnp.mean(rows, axis=-1, keepdims=True)
    inverse = lax.rsqrt(jnp.mean(center * center, axis=-1, keepdims=True) + EPS)
    return center * inverse, inverse


def iota(shape, axis):
    return lax.broadcasted_iota(jnp.int32, shape, axis)


names = []


def ident(name):
    if name not in names:
        names.append(name)
    return names.index(name)


N_REMOTE = 128
N_LOCAL = 32


def kernel(
    tokens_h, targets_h, vis_ref, wqkv_h, wout_h, wembed_h, mtok_ref, dpos_h, wup_h, wdown_h, whead_h,
    sums_ref,
    tokens, targets, wq, wk, wv, wout, wembed, dpos, wup, wdown, whead,
    selector, seen_col, packed, heads, other, kv_own, kv_r, kv_l, keys, vals, qx, acc, top,
    att_out, att_in, att, att_sib, pos_slot, tgt_slot, mask_slot,
    unit_m, act_m, og_m, hg_m, unit_ms, act_ms, og_ms, hg_ms, gd_acc, gu_acc,
    unit_v, act_v, og_v, hg_v, sg_v, unit_vs, act_vs, og_vs, hg_vs, sg_vs,
    rs_gd, rs_gu, rs_g, rs_h, rs_x2, rs_y2,
    in_gd, in_gu, in_g, in_h, in_x2, in_y2,
    zs, zr, zg, zgr, ag, gr,
    send_sem, recv_sem, load_sem,
):
    dp = lax.axis_index("dp")
    seg = lax.axis_index("segment")
    blk = lax.axis_index("blk")
    x, core = dp // 2, dp % 2
    y, z = seg * 2 + blk // 8, blk % 8
    y_lo = blk // 8

    def device(px, pc, py, pz):
        return (px * 2 + pc, py // 2, (py % 2) * 8 + pz)

    def at_x(step):
        return device((x + step + 4) % 4, core, y, z)

    def at_y(step):
        return device(x, core, (y + step + 4) % 4, z)

    def at_z(step):
        return device(x, core, y, (z + step + 8) % 8)

    sibling = device(x, 1 - core, y, z)

    loads = {}

    def load(name, src, dst):
        copy = pltpu.make_async_copy(src, dst, load_sem.at[len(loads)])
        copy.start()
        loads[name] = copy

    load("tokens", tokens_h, tokens)
    for name, dst, first in (("wk", wk, 640), ("wv", wv, 1280), ("wq", wq, 0)):
        for part in range(2):
            span = pl.ds(part * 640, 640)
            load(name + str(part), wqkv_h.at[span, pl.ds(first, 640)], dst.at[span])

    barrier = pltpu.get_barrier_semaphore()
    peers = [at_z(step) for step in range(1, 8)]
    for px in range(4):
        for pc in range(2):
            for py in range(4):
                if px or pc or py:
                    peers.append(device((x + px) % 4, (core + pc) % 2, (y + py) % 4, z))
    for peer in peers:
        pl.semaphore_signal(barrier, inc=1, device_id=peer, device_id_type=MESH)

    started = []

    def describe(name, src, dst, target, landed=None):
        return pltpu.make_async_remote_copy(
            src_ref=src,
            dst_ref=dst,
            send_sem=send_sem.at[ident(name)],
            recv_sem=recv_sem.at[ident(landed or name)],
            device_id=target,
            device_id_type=MESH,
        )

    def send(name, src, dst, target):
        copy = describe(name, src, dst, target)
        copy.start()
        started.append(copy)
        return copy

    vis = vis_ref[...].astype(F32)
    tri = (iota((TILE, TILE), 0) <= iota((TILE, TILE), 1)).astype(F32).astype(BF16)
    vis8 = jnp.broadcast_to(vis, (8, TILE))
    position = dot(vis8.astype(BF16), tri)[0:1, :] - 1.0
    count = jnp.sum(vis, axis=1, keepdims=True)
    slot_ids = iota((ROWS, TILE), 0).astype(F32)
    chosen = jnp.where((position == slot_ids) & (vis > 0.5), 1.0, 0.0).astype(BF16)
    selector[...] = chosen
    loads["tokens"].wait()
    rows = dot(chosen, tokens[...])
    packed[...] = rows.astype(BF16)
    normed = normalize(rows)[0].astype(BF16)
    seen_col[...] = dot_tn(chosen, jnp.ones((ROWS, 128), BF16))
    projected = []
    for name, weight in (("wk", wk), ("wv", wv), ("wq", wq)):
        loads[name + "0"].wait()
        loads[name + "1"].wait()
        projected.append(dot(normed, weight[...]))
    load("dpos", dpos_h, dpos)
    load("targets", targets_h, targets)
    load("wup", wup_h, wup)
    load("wdown", wdown_h, wdown)
    load("whead", whead_h, whead)
    load("wout", wout_h, wout)
    load("wembed", wembed_h, wembed)
    slot_row = iota((ROWS, 256), 0)
    for h in range(HEADS):
        parts = [p[:, h * 80 : h * 80 + 80] for p in projected]
        block = jnp.concatenate(parts + [jnp.zeros((ROWS, 16), F32)], axis=1)
        block = jnp.where(slot_row >= CAP, count, block)
        heads[h] = block.astype(BF16)

    pl.semaphore_wait(barrier, len(peers))
    up_head = ((y + 1) % 4) * 2
    down_head = ((y + 3) % 4) * 2 + 1
    from_down = send("qkv+", heads.at[up_head], other.at[0], at_y(1))
    from_up = send("qkv-", heads.at[down_head], other.at[1], at_y(-1))

    lane = iota((ROWS, 128), 1)
    slot128 = iota((ROWS, 128), 0).astype(F32)

    def make_query(block, j, first):
        window = pltpu.roll(block[:, 128:256].astype(F32), 96, 1)
        query = jnp.where(lane < 80, window, jnp.where(lane == 80, 1.0, 0.0))
        qx[j, first : first + ROWS, :] = query.astype(BF16)

    lane88 = iota((ROWS // 2, 128), 1)

    def fold(first, second, part):
        both = jnp.concatenate(
            [first[:, 0:160].astype(F32), second[:, 0:160].astype(F32), jnp.zeros((ROWS, 64), F32)],
            axis=1,
        )
        third = both[:, 256:384]
        third = jnp.where(lane88 < 64, third[0:88], pltpu.roll(third[88:ROWS], 64, 1))
        part[0:ROWS, :] = both[:, 0:128].astype(BF16)
        part[ROWS : 2 * ROWS, :] = both[:, 128:256].astype(BF16)
        third = jnp.concatenate([third, jnp.zeros((8, 128), F32)], axis=0)
        part[2 * ROWS : PART, :] = third.astype(BF16)

    def unfold(part, first):
        p0 = part[0:ROWS, :].astype(F32)
        p1 = part[ROWS : 2 * ROWS, :].astype(F32)
        third = part[2 * ROWS : PART, :].astype(F32)[0:88]
        p2 = jnp.concatenate([third, pltpu.roll(third, 64, 1)], axis=0)
        pairs = (
            (p0, pltpu.roll(jnp.concatenate([p0, p1], axis=1), 176, 1)),
            (pltpu.roll(p1, 96, 1), pltpu.roll(jnp.concatenate([p1, p2], axis=1), 144, 1)),
        )
        for j in range(2):
            key, value = pairs[j]
            counts = key[CAP : CAP + 1, :]
            outside = jnp.where((lane == 80) & (slot128 >= counts), OUT_MASK, 0.0)
            keys[j, first : first + ROWS, :] = jnp.where(lane < 80, key, outside).astype(BF16)
            vals[j, first : first + ROWS, :] = jnp.where(
                lane == 80, 1.0, value[:, 0:128]
            ).astype(BF16)

    ring = {}

    def ring_start(part):
        ring["r", part, 0] = send("r0%d" % part, kv_own.at[part], kv_r.at[part, 0], at_z(1))
        ring["l", part, 0] = send("l0%d" % part, kv_own.at[part], kv_l.at[part, 0], at_z(-1))

    def ring_next(part, step):
        for way, buffer, to in (("r", kv_r, 1), ("l", kv_l, -1)):
            ring[way, part, step].wait_recv()
            if step < 2 or (step == 2 and (way == "r") == (part == 0)):
                ring[way, part, step + 1] = send(
                    "%s%d%d" % (way, step + 1, part),
                    buffer.at[part, step],
                    buffer.at[part, step + 1],
                    at_z(to),
                )

    own = [heads[y * 2], heads[y * 2 + 1]]
    fold(own[0], own[1], kv_own.at[0])
    ring_start(0)
    for j in range(2):
        make_query(own[j], j, 0)
    from_down.wait_recv()
    from_up.wait_recv()
    others = [other[0], other[1]]
    fold(others[0], others[1], kv_own.at[1])
    ring_start(1)
    for j in range(2):
        make_query(others[j], j, ROWS)

    scale = math.log2(math.e) / math.sqrt(HEAD_DIM)

    def attend_head(j, first, begin=False):
        span = slice(first, first + 2 * ROWS)
        scores = dot_nt(qx[j], keys[j, span, :])
        best = jnp.max(scores, axis=1, keepdims=True)
        if not begin:
            before = top[j]
            best = jnp.maximum(before[:, 0:1], best)
        probs = jnp.exp2((scores - best) * scale).astype(BF16)
        term = dot(probs, vals[j, span, :])
        if not begin:
            term = term + acc[j] * jnp.exp2((before - best) * scale)
        acc[j] = term
        top[j] = jnp.broadcast_to(best, (2 * ROWS, 128))

    def attend(first, one, two, begin=False):
        unfold(one, first)
        unfold(two, first + ROWS)
        for j in range(2):
            attend_head(j, first, begin)

    grad_scale = 8.0 / math.sqrt(8 * 16 * (TILE - VIS_TILE))
    root_half = 1.0 / math.sqrt(2.0)
    order = iota((DEC, DEC), 1)
    source = (order // 32 % 4) * 128 + (order // 256) * 64 + (order // 128 % 2) * 32 + order % 32
    shuffle = (iota((DEC, DEC), 0) == source).astype(F32).astype(BF16)

    def decode_forward(stream, goal, keep, unit, act, ready):
        normal, inverse = normalize(stream)
        low = normal.astype(BF16)
        unit[...] = low
        hidden = dot(low, wup[...])
        cumulative = 0.5 * (1.0 + lax.erf(hidden * root_half))
        active = (hidden * cumulative).astype(BF16)
        act[...] = active
        ready()
        slope = cumulative + hidden * jnp.exp(-0.5 * hidden * hidden) * (
            1.0 / math.sqrt(2.0 * math.pi)
        )
        stream_out = stream + dot(active, wdown[...])
        predicted = dot_nt(stream_out.astype(BF16), whead[...])
        pred_grad = ((predicted - goal) * (keep * grad_scale)).astype(BF16)
        out_grad = dot(pred_grad, whead[...])
        return normal, inverse, slope, out_grad

    def decode_hidden(out_low, slope, hg):
        hidden_grad = (dot_nt(out_low, wdown[...]) * slope).astype(BF16)
        for c in range(2):
            for px in range(4):
                at = px * 256 + c * 128
                hg[c, :, px * 128 : px * 128 + 128] = hidden_grad[:, at : at + 128]
        return hidden_grad

    def split_out(out_low, og):
        mixed = dot(out_low, shuffle).astype(BF16)
        og[0] = mixed[:, 0:256]
        og[1] = mixed[:, 256:512]

    attend(0, kv_own.at[0], kv_own.at[1], begin=True)
    for name in ("dpos", "targets", "wup", "wdown", "whead"):
        loads[name].wait()
    ring_next(0, 0)
    part_rows = pl.ds(pl.multiple_of(seg * HALF, 16), HALF)
    stream_m = mtok_ref[...].astype(F32)[None, :] + dpos[part_rows, :].astype(F32)
    patch = iota((HALF, TILE), 0) + seg * HALF
    pick = (iota((HALF, TILE), 1) == patch).astype(F32).astype(BF16)
    goal_m = dot_nt(pick, targets[...])
    keep_m = 1.0 - seen_col[part_rows, :][:, 0:1]
    masked = []

    def ready_m():
        masked.append(send("unit_m", unit_m, unit_ms, sibling))
        masked.append(send("act_m", act_m, act_ms, sibling))
        ring_next(1, 0)

    normal, inverse, slope, out_grad = decode_forward(
        stream_m, goal_m, keep_m, unit_m, act_m, ready_m
    )
    attend(2 * ROWS, kv_r.at[0, 0], kv_l.at[0, 0])
    ring_next(0, 1)
    out_low = out_grad.astype(BF16)
    split_out(out_low, og_m)
    masked.append(send("og_m", og_m.at[1 - core], og_ms, sibling))
    decode_hidden(out_low, slope, hg_m)
    masked.append(send("hg_m", hg_m.at[1 - core], hg_ms, sibling))
    attend(4 * ROWS, kv_r.at[1, 0], kv_l.at[1, 0])
    ring_next(1, 1)
    attend(6 * ROWS, kv_r.at[0, 1], kv_l.at[0, 1])
    slot_first = pl.multiple_of(seg * SEG_STEP, 16)
    slot_rows = pl.ds(slot_first, SLOTS)
    chosen_part = selector[slot_rows, :]
    pos_slot[...] = dot(chosen_part, dpos[...])
    tgt_slot[...] = dot_nt(chosen_part, targets[...])
    number = iota((SLOTS, 128), 0) + seg * SEG_STEP
    kept = (number.astype(F32) < count) & (number >= seg * SLOTS)
    mask_slot[...] = jnp.where(kept, 1.0, 0.0)
    ring_next(0, 2)
    attend(8 * ROWS, kv_r.at[1, 1], kv_l.at[1, 1])
    for copy in masked:
        copy.wait_recv()
    gd_acc[...] = dot_tn(og_m[core], act_m[...]) + dot_tn(og_ms[...], act_ms[...])
    ring_next(1, 2)
    attend(10 * ROWS, kv_r.at[0, 2], kv_l.at[0, 2])
    gu_acc[...] = dot_tn(unit_m[...], hg_m[core]) + dot_tn(unit_ms[...], hg_ms[...])
    attend(12 * ROWS, kv_r.at[1, 2], kv_l.at[1, 2])
    loads["wout"].wait()
    loads["wembed"].wait()
    ring["r", 0, 3].wait_recv()
    ring["l", 1, 3].wait_recv()
    unfold(kv_r.at[0, 3], 14 * ROWS)
    unfold(kv_l.at[1, 3], 15 * ROWS)

    back = []
    for j in range(2):
        attend_head(j, 14 * ROWS)
        total = acc[j]
        done = (total * (1.0 / total[:, 80:81])).astype(BF16)
        att_out[j, 0] = done[0:ROWS]
        att_out[j, 1] = done[ROWS : 2 * ROWS]
        for step, i in ((2, 0), (1, 1), (-1, 1)):
            goal_seg = ((y + step + 4) % 4) // 2
            span = pl.ds(pl.multiple_of(goal_seg * SEG_STEP, 16), SLOTS)
            back.append(
                send("b%d%d" % (j, step + 4), att_out.at[j, i, span], att_in.at[y, j], at_y(step))
            )
        att_in[y, j] = att_out[j, 0, slot_rows, :]
    for copy in back:
        copy.wait_recv()
    pieces = [att_in[i // 2, i % 2][:, 0:80].astype(F32) for i in range(HEADS)]
    for c in range(2):
        att[c] = jnp.concatenate(pieces[c * 4 : c * 4 + 4], axis=1).astype(BF16)
    swap_att = send("att_s", att.at[1 - core], att_sib, sibling)
    attended = jnp.concatenate(pieces, axis=1).astype(BF16)

    encoded = packed[slot_rows, :].astype(F32) + dot(attended, wout[...])
    embedded = dot(encoded.astype(BF16), wembed[...])
    stream_v = embedded + pos_slot[...]
    swap = {}

    def ready_v():
        swap["unit"] = send("unit_v", unit_v, unit_vs, sibling)
        swap["act"] = send("act_v", act_v, act_vs, sibling)

    normal, inverse, slope, out_grad = decode_forward(
        stream_v, tgt_slot[...], mask_slot[:, 0:1], unit_v, act_v, ready_v
    )
    out_low = out_grad.astype(BF16)
    split_out(out_low, og_v)
    swap["og"] = send("og_v", og_v.at[1 - core], og_vs, sibling)
    hidden_grad = decode_hidden(out_low, slope, hg_v)
    swap["hg"] = send("hg_v", hg_v.at[1 - core], hg_vs, sibling)

    def ring_sum(name, chunks, landing, h0, h1, place, at):
        right, left, far = (place + 1) % 4, (place + 3) % 4, (place + 2) % 4
        s0, s1 = pl.ds(0, h0), pl.ds(h0, h1)
        rel0 = send(name + "rel0", chunks.at[far, s0], landing.at[0, s0], at(1))
        rel1 = send(name + "rel1", chunks.at[far, s1], landing.at[0, s1], at(-1))
        dir1 = send(name + "dir1", chunks.at[right, s1], landing.at[1, s1], at(1))
        dir0 = send(name + "dir0", chunks.at[left, s0], landing.at[1, s0], at(-1))
        state = {}

        def relay():
            rel0.wait_recv()
            landing[3, s0, :] = (
                landing[0, s0, :].astype(F32) + chunks[right, s0, :].astype(F32)
            ).astype(BF16)
            state["c0"] = send(name + "c0", landing.at[3, s0], landing.at[2, s0], at(1))
            rel1.wait_recv()
            landing[3, s1, :] = (
                landing[0, s1, :].astype(F32) + chunks[left, s1, :].astype(F32)
            ).astype(BF16)
            state["c1"] = send(name + "c1", landing.at[3, s1], landing.at[2, s1], at(-1))

        def finish():
            dir0.wait_recv()
            dir1.wait_recv()
            state["c0"].wait_recv()
            state["c1"].wait_recv()
            return (
                chunks[place].astype(F32) + landing[1].astype(F32) + landing[2].astype(F32)
            )

        return relay, finish

    swap["act"].wait_recv()
    swap["og"].wait_recv()
    gd_t = gd_acc[...] + dot_tn(og_v[core], act_v[...]) + dot_tn(og_vs[...], act_vs[...])
    gd_t = gd_t.astype(BF16)
    for py in range(4):
        for px in range(4):
            for k in range(4):
                r = (py // 2) * 128 + px * 32
                c = (py % 2) * 512 + k * 128
                at = px * 128 + k * 32
                rs_gd[py, at : at + 32, :] = gd_t[r : r + 32, c : c + 128]
    relay_gd, finish_gd = ring_sum("gd", rs_gd, in_gd, 256, 256, y, at_y)

    unit_grad = dot_nt(hidden_grad, wup[...])
    cross = jnp.mean(unit_grad * normal, axis=-1, keepdims=True)
    middle = jnp.mean(unit_grad, axis=-1, keepdims=True)
    stream_grad = out_grad + inverse * (unit_grad - middle - normal * cross)
    sg_v[...] = stream_grad.astype(BF16)
    swap["sg"] = send("sg_v", sg_v, sg_vs, sibling)

    swap["unit"].wait_recv()
    swap["hg"].wait_recv()
    gu_t = gu_acc[...] + dot_tn(unit_v[...], hg_v[core]) + dot_tn(unit_vs[...], hg_vs[...])
    gu_t = gu_t.astype(BF16)
    for px in range(4):
        rs_gu[px] = gu_t[:, px * 128 : px * 128 + 128]
    relay_gu, finish_gu = ring_sum("gu", rs_gu, in_gu, 256, 256, x, at_x)

    swap_att.wait_recv()
    swap["sg"].wait_recv()
    inner = dot_tn(att[core], sg_v[...]) + dot_tn(att_sib[...], sg_vs[...])
    inner = inner.astype(BF16)
    for px in range(4):
        for i in range(4):
            rs_g[px, 48 * i : 48 * i + 48, :] = inner[80 * i : 80 * i + 48, px * 128 : px * 128 + 128]
            rs_h[i, 32 * px : 32 * px + 32, :] = inner[
                80 * i + 48 : 80 * i + 80, px * 128 : px * 128 + 128
            ]
    relay_g, finish_g = ring_sum("g", rs_g, in_g, 96, 96, x, at_x)
    relay_h, finish_h = ring_sum("h", rs_h, in_h, 64, 64, y, at_y)

    relay_gd()
    relay_gu()
    relay_g()
    relay_h()

    gd_1 = finish_gd()
    h_1 = finish_h()
    for px in range(4):
        rs_y2[px, 0:128, :] = gd_1[px * 128 : px * 128 + 128].astype(BF16)
        rs_y2[px, 128:160, :] = h_1[px * 32 : px * 32 + 32].astype(BF16)
    relay_y2, finish_y2 = ring_sum("y2", rs_y2, in_y2, 80, 80, x, at_x)
    gu_1 = finish_gu()
    g_1 = finish_g()
    lane128 = iota((128, 128), 1)
    for py in range(4):
        first = gu_1[(py % 2) * 256 : (py % 2) * 256 + 128]
        second = gu_1[(py % 2) * 256 + 128 : (py % 2) * 256 + 256]
        if py // 2 == 0:
            pair = jnp.where(lane128 < 64, first, pltpu.roll(second, 64, 1))
        else:
            pair = jnp.where(lane128 < 64, pltpu.roll(first, 64, 1), second)
        rs_x2[py, 0:128, :] = pair.astype(BF16)
        rs_x2[py, 128:176, :] = g_1[py * 48 : py * 48 + 48].astype(BF16)
    relay_x2, finish_x2 = ring_sum("x2", rs_x2, in_x2, 96, 80, y, at_y)
    relay_y2()
    relay_x2()
    y_2 = finish_y2()
    x_2 = finish_x2()

    zg[0] = x_2[128:176].astype(BF16)
    zg[1] = jnp.concatenate([x_2[160:176], y_2[128:160]], axis=0).astype(BF16)
    holder = z // 2 == y
    inner_copies = []
    for step in range(1, 8):
        to = (z + step) % 8
        copy = describe("zg%d" % step, zg.at[to % 2], zgr.at[step - 1], at_z(step))
        goes = to // 2 == y
        pl.when(goes)(copy.start)
        inner_copies.append((copy, goes))
    lane32 = iota((32, 128), 1)
    for pz in range(8):
        up = x_2[(pz % 4) * 32 : (pz % 4) * 32 + 32]
        if pz // 4 == 1:
            up = pltpu.roll(up, 64, 1)
        down = y_2[(pz // 2) * 32 : (pz // 2) * 32 + 32]
        if pz % 2 == 0:
            down = pltpu.roll(down, 64, 1)
        zs[pz] = jnp.where(lane32 < 64, up, down).astype(BF16)
    last = []
    for step in range(1, 8):
        last.append(send("z%d" % step, zs.at[(z + step) % 8], zr.at[step - 1], at_z(step)))

    spread = []
    for step in range(4):
        for pc in range(2):
            for half in range(2):
                target = device((x + step) % 4, pc, core + 2 * half, z)
                copy = describe("ag%d%d%d" % (step, pc, half), ag, gr.at[x], target, "ag%d" % step)
                goes = holder
                if step == 0:
                    goes = holder & ((core != pc) | (y != core + 2 * half))
                spread.append((copy, goes))

    @pl.when(holder)
    def _():
        total = zg[z % 2].astype(F32)
        for step in range(1, 8):
            inner_copies[step - 1][0].wait_recv()
            total = total + zgr[step - 1].astype(F32)
        ag[...] = total.astype(BF16)

    for copy, goes in spread:
        pl.when(goes)(copy.start)
    mine = holder & (core == y_lo)

    @pl.when(mine)
    def _():
        gr[x] = ag[...]

    result = zs[z].astype(F32)
    for step in range(1, 8):
        last[step - 1].wait_recv()
        result = result + zr[step - 1].astype(F32)
    sums_ref[0:32, :] = result
    pl.when(jnp.logical_not(mine))(spread[0][0].wait_recv)
    for step in range(1, 4):
        spread[step * 4][0].wait_recv()
    rows_b = jnp.concatenate([gr[i] for i in range(4)], axis=1)
    columns = pl.ds(pl.multiple_of((x * 4 + core * 2 + seg) * 80, 16), 80)
    product = dot_nt(rows_b, wembed[columns, :])
    product = jnp.where(z % 2 == 0, product[0:40], product[8:48])
    sums_ref[32:72, 0:80] = product
    for copy, goes in inner_copies + spread:
        pl.when(goes)(copy.wait_send)
    for copy in started:
        copy.wait_send()


def split_sums(sums_ref, go_ref, gu_ref, gd_ref):
    go_ref[...] = sums_ref[32:72, 0:80]
    gu_ref[...] = sums_ref[0:32, 0:64]
    gd_ref[...] = pltpu.roll(sums_ref[0:32, :], 64, 1)[:, 0:64]


def on_device(
    tokens, targets, visible, w_qkv, w_out, w_embed, mask_token, dec_pos, w_up, w_down, w_head
):
    names.clear()
    anywhere = pl.BlockSpec(memory_space=pl.ANY)
    vmem = pl.BlockSpec(memory_space=pltpu.VMEM)

    def low(*shape):
        return pltpu.VMEM(shape, BF16)

    def wide(*shape):
        return pltpu.VMEM(shape, F32)

    scratch = [
        low(TILE, D), low(PIX, TILE), low(D, INNER), low(D, INNER), low(D, INNER), low(INNER, D),
        low(D, DEC), low(TILE, DEC), low(DEC, FF), low(FF, DEC), low(PIX, DEC),
        low(ROWS, TILE), wide(TILE, 128), low(ROWS, D), low(HEADS, ROWS, 256), low(2, ROWS, 256),
        low(2, PART, 128), low(2, 4, PART, 128), low(2, 4, PART, 128),
        low(2, 16 * ROWS, 128), low(2, 16 * ROWS, 128), low(2, 2 * ROWS, 128),
        wide(2, 2 * ROWS, 128), wide(2, 2 * ROWS, 128),
        low(2, 2, ROWS, 128), low(4, 2, SLOTS, 128), low(2, SLOTS, 320), low(SLOTS, 320),
        wide(SLOTS, DEC), wide(SLOTS, PIX), wide(SLOTS, 128),
        low(HALF, DEC), low(HALF, FF), low(2, HALF, 256), low(2, HALF, DEC),
        low(HALF, DEC), low(HALF, FF), low(HALF, 256), low(HALF, DEC),
        wide(256, FF), wide(DEC, DEC),
        low(SLOTS, DEC), low(SLOTS, FF), low(2, SLOTS, 256), low(2, SLOTS, DEC), low(SLOTS, DEC),
        low(SLOTS, DEC), low(SLOTS, FF), low(SLOTS, 256), low(SLOTS, DEC), low(SLOTS, DEC),
        low(4, 512, 128), low(4, 512, 128), low(4, 192, 128), low(4, 128, 128),
        low(4, 176, 128), low(4, 160, 128),
        low(4, 512, 128), low(4, 512, 128), low(4, 192, 128), low(4, 128, 128),
        low(4, 176, 128), low(4, 160, 128),
        low(8, 32, 128), low(7, 32, 128), low(2, 48, 128), low(7, 48, 128), low(48, 128),
        low(4, 48, 128),
        pltpu.SemaphoreType.DMA((N_REMOTE,)),
        pltpu.SemaphoreType.DMA((N_REMOTE,)),
        pltpu.SemaphoreType.DMA((N_LOCAL,)),
    ]
    sums = pl.pallas_call(
        kernel,
        out_shape=jax.ShapeDtypeStruct((80, 128), F32),
        in_specs=[
            anywhere, anywhere, vmem, anywhere, anywhere, anywhere, vmem, anywhere, anywhere,
            anywhere, anywhere,
        ],
        out_specs=vmem,
        scratch_shapes=scratch,
        compiler_params=pltpu.CompilerParams(
            collective_id=0, has_side_effects=True, vmem_limit_bytes=56 * 1024 * 1024
        ),
    )(
        tokens[0], targets[0].T, visible, w_qkv, w_out, w_embed, mask_token, dec_pos, w_up,
        w_down, w_head.T,
    )
    grad_out, grad_up, grad_down = pl.pallas_call(
        split_sums,
        out_shape=(
            jax.ShapeDtypeStruct((40, 80), F32),
            jax.ShapeDtypeStruct((32, 64), F32),
            jax.ShapeDtypeStruct((32, 64), F32),
        ),
        in_specs=[vmem],
        out_specs=(vmem, vmem, vmem),
    )(sums)
    return grad_out, grad_up, grad_down.T


def solution(mesh):
    in_specs = (
        P("dp", "blk", None),
        P("dp", "blk", None),
        P("dp", "blk"),
        P(),
        P(),
        P(),
        P(),
        P("blk", None),
        P(),
        P(),
        P(),
    )
    out_specs = (
        P("blk", ("dp", "segment")),
        P("blk", ("dp", "segment")),
        P("blk", ("dp", "segment")),
    )
    return jax.shard_map(
        on_device, mesh=mesh, in_specs=in_specs, out_specs=out_specs, check_vma=False
    )
```

time: 82.4 us -> 76 us (0.922)
  the two profiles are of different devices: /device:TPU:8 before, /device:TPU:1 now
where the time goes in v2:
time: 76 us; the launch traced here: 75.9 us
  Pallas kernels  75.2 us (99%)
    pallas_call x1, Pallas kernels, on_device(): pl.pallas_call(kernel, out_shape=jax.ShapeDtypeStruct((80, 128), F32), in...  73.8 us

profile of v2, /device:TPU:1, one launch (start us, length us, event | category | flops | bytes accessed | tf_op | source)
XLA Modules:
  0.0 75.9 jit_solution(12579162456348896824)
XLA Ops:
  0.6 73.8 %shard_map.130.sums_ref = f32[80,128]{1,0:T(8,128)} custom-call(bf16[384,1280]{1,0:T(8,128)(2,1)} %bitcast.7, bf16[1176,384]{1,0:T(8,128)(2,1)} %bitcast.8, s32[1,384]{1,0:T(1,128)} %vis_ref.1, bf16[1280,1920]{1,0:T(8,128)(2,1)} %wqkv_h.1, bf16[640,1280]{1,0:T(8,128)(2,1)} %wout_h.1, bf16[1280,512]{1,0:T(8,128)(2,1)} %wembed_h.1, bf16[512]{0:T(512)(128)(2,1)} %mtok_ref.1, ...), custom_call_target="tpu_custom_call" | custom-call | tf_op jit(solution)/shard_map/pallas_call | solution.py:618
  74.4 1.5 %shard_map.131 = (f32[40,80]{1,0:T(8,128)}, f32[32,64]{1,0:T(8,128)}, f32[32,64]{1,0:T(8,128)}) custom-call(f32[80,128]{1,0:T(8,128)} %shard_map.130.sums_ref), custom_call_target="tpu_custom_call" | custom-call | tf_op jit(solution)/shard_map/pallas_call | solution.py:634

commit v3 on v2

--- a/solution.py
+++ b/solution.py
@@ -61,8 +61,9 @@
     return names.index(name)
 
 
-N_REMOTE = 128
-N_LOCAL = 32
+N_SEND = 32
+N_RECV = 88
+N_LOCAL = 14
 
 
 def kernel(
@@ -73,8 +74,8 @@
     att_out, att_in, att, att_sib, pos_slot, tgt_slot, mask_slot,
     unit_m, act_m, og_m, hg_m, unit_ms, act_ms, og_ms, hg_ms, gd_acc, gu_acc,
     unit_v, act_v, og_v, hg_v, sg_v, unit_vs, act_vs, og_vs, hg_vs, sg_vs,
-    rs_gd, rs_gu, rs_g, rs_h, rs_x2, rs_y2,
-    in_gd, in_gu, in_g, in_h, in_x2, in_y2,
+    rs_gd, rs_gu, rs_g, rs_h, rs_gd2, rs_gu2, rs_g2, rs_h2,
+    in_gd, in_gu, in_g, in_h, in_gd2, in_gu2, in_g2, in_h2,
     zs, zr, zg, zgr, ag, gr,
     send_sem, recv_sem, load_sem,
 ):
@@ -113,29 +114,41 @@
             load(name + str(part), wqkv_h.at[span, pl.ds(first, 640)], dst.at[span])
 
     barrier = pltpu.get_barrier_semaphore()
-    peers = [at_z(step) for step in range(1, 8)]
-    for px in range(4):
-        for pc in range(2):
-            for py in range(4):
-                if px or pc or py:
-                    peers.append(device((x + px) % 4, (core + pc) % 2, (y + py) % 4, z))
+    holder = z // 2 == y
+    mine = holder & (core == y_lo)
+    peers = [sibling] + [at_z(step) for step in range(1, 8)]
+    peers += [at_x(step) for step in range(1, 4)] + [at_y(step) for step in range(1, 4)]
     for peer in peers:
         pl.semaphore_signal(barrier, inc=1, device_id=peer, device_id_type=MESH)
+    for step in range(4):
+        source = device((x + step) % 4, y_lo, z // 2, z)
+
+        def greet():
+            pl.semaphore_signal(barrier, inc=1, device_id=source, device_id_type=MESH)
+
+        if step == 0:
+            pl.when(jnp.logical_not(mine))(greet)
+        else:
+            greet()
+    greetings = len(peers) + jnp.where(holder, 16, 0) - jnp.where(mine, 1, 0)
 
     started = []
 
-    def describe(name, src, dst, target, landed=None):
+    def describe(src, dst, target, slot, name):
         return pltpu.make_async_remote_copy(
             src_ref=src,
             dst_ref=dst,
-            send_sem=send_sem.at[ident(name)],
-            recv_sem=recv_sem.at[ident(landed or name)],
+            send_sem=send_sem.at[slot],
+            recv_sem=recv_sem.at[ident(name)],
             device_id=target,
             device_id_type=MESH,
         )
 
     def send(name, src, dst, target):
-        copy = describe(name, src, dst, target)
+        count = len(started)
+        if count >= N_SEND:
+            started[count - N_SEND].wait_send()
+        copy = describe(src, dst, target, count % N_SEND, name)
         copy.start()
         started.append(copy)
         return copy
@@ -172,7 +185,7 @@
         block = jnp.where(slot_row >= CAP, count, block)
         heads[h] = block.astype(BF16)
 
-    pl.semaphore_wait(barrier, len(peers))
+    pl.semaphore_wait(barrier, greetings)
     up_head = ((y + 1) % 4) * 2
     down_head = ((y + 3) % 4) * 2 + 1
     from_down = send("qkv+", heads.at[up_head], other.at[0], at_y(1))
@@ -219,21 +232,29 @@
             ).astype(BF16)
 
     ring = {}
+    ring_halves = (pl.ds(0, PART // 2), pl.ds(PART // 2, PART // 2))
+
+    def ring_send(way, part, step, half, src):
+        buffer, to = (kv_r, 1) if way == "r" else (kv_l, -1)
+        rows_of = ring_halves[half]
+        ring[way, part, step, half] = send(
+            "%s%d%d%d" % (way, step, part, half),
+            src.at[rows_of],
+            buffer.at[part, step, rows_of],
+            at_z(to),
+        )
 
     def ring_start(part):
-        ring["r", part, 0] = send("r0%d" % part, kv_own.at[part], kv_r.at[part, 0], at_z(1))
-        ring["l", part, 0] = send("l0%d" % part, kv_own.at[part], kv_l.at[part, 0], at_z(-1))
+        for half in range(2):
+            for way in "rl":
+                ring_send(way, part, 0, half, kv_own.at[part])
 
     def ring_next(part, step):
-        for way, buffer, to in (("r", kv_r, 1), ("l", kv_l, -1)):
-            ring[way, part, step].wait_recv()
-            if step < 2 or (step == 2 and (way == "r") == (part == 0)):
-                ring[way, part, step + 1] = send(
-                    "%s%d%d" % (way, step + 1, part),
-                    buffer.at[part, step],
-                    buffer.at[part, step + 1],
-                    at_z(to),
-                )
+        for half in range(2):
+            for way, buffer in (("r", kv_r), ("l", kv_l)):
+                ring[way, part, step, half].wait_recv()
+                if step < 2 or (step == 2 and (way == "r") == (part == 0)):
+                    ring_send(way, part, step + 1, half, buffer.at[part, step])
 
     own = [heads[y * 2], heads[y * 2 + 1]]
     fold(own[0], own[1], kv_own.at[0])
@@ -356,8 +377,9 @@
     attend(12 * ROWS, kv_r.at[1, 2], kv_l.at[1, 2])
     loads["wout"].wait()
     loads["wembed"].wait()
-    ring["r", 0, 3].wait_recv()
-    ring["l", 1, 3].wait_recv()
+    for half in range(2):
+        ring["r", 0, 3, half].wait_recv()
+        ring["l", 1, 3, half].wait_recv()
     unfold(kv_r.at[0, 3], 14 * ROWS)
     unfold(kv_l.at[1, 3], 15 * ROWS)
 
@@ -401,37 +423,20 @@
     hidden_grad = decode_hidden(out_low, slope, hg_v)
     swap["hg"] = send("hg_v", hg_v.at[1 - core], hg_vs, sibling)
 
-    def ring_sum(name, chunks, landing, h0, h1, place, at):
-        right, left, far = (place + 1) % 4, (place + 3) % 4, (place + 2) % 4
-        s0, s1 = pl.ds(0, h0), pl.ds(h0, h1)
-        rel0 = send(name + "rel0", chunks.at[far, s0], landing.at[0, s0], at(1))
-        rel1 = send(name + "rel1", chunks.at[far, s1], landing.at[0, s1], at(-1))
-        dir1 = send(name + "dir1", chunks.at[right, s1], landing.at[1, s1], at(1))
-        dir0 = send(name + "dir0", chunks.at[left, s0], landing.at[1, s0], at(-1))
-        state = {}
-
-        def relay():
-            rel0.wait_recv()
-            landing[3, s0, :] = (
-                landing[0, s0, :].astype(F32) + chunks[right, s0, :].astype(F32)
-            ).astype(BF16)
-            state["c0"] = send(name + "c0", landing.at[3, s0], landing.at[2, s0], at(1))
-            rel1.wait_recv()
-            landing[3, s1, :] = (
-                landing[0, s1, :].astype(F32) + chunks[left, s1, :].astype(F32)
-            ).astype(BF16)
-            state["c1"] = send(name + "c1", landing.at[3, s1], landing.at[2, s1], at(-1))
+    def direct_sum(name, chunks, landing, place, at):
+        copies = [
+            send(name + str(step), chunks.at[(place + step) % 4], landing.at[step - 1], at(step))
+            for step in range(1, 4)
+        ]
 
         def finish():
-            dir0.wait_recv()
-            dir1.wait_recv()
-            state["c0"].wait_recv()
-            state["c1"].wait_recv()
-            return (
-                chunks[place].astype(F32) + landing[1].astype(F32) + landing[2].astype(F32)
-            )
-
-        return relay, finish
+            total = chunks[place].astype(F32)
+            for step in range(3):
+                copies[step].wait_recv()
+                total = total + landing[step].astype(F32)
+            return total
+
+        return finish
 
     swap["act"].wait_recv()
     swap["og"].wait_recv()
@@ -444,7 +449,7 @@
                 c = (py % 2) * 512 + k * 128
                 at = px * 128 + k * 32
                 rs_gd[py, at : at + 32, :] = gd_t[r : r + 32, c : c + 128]
-    relay_gd, finish_gd = ring_sum("gd", rs_gd, in_gd, 256, 256, y, at_y)
+    finish_gd = direct_sum("gd", rs_gd, in_gd, y, at_y)
 
     unit_grad = dot_nt(hidden_grad, wup[...])
     cross = jnp.mean(unit_grad * normal, axis=-1, keepdims=True)
@@ -459,7 +464,6 @@
     gu_t = gu_t.astype(BF16)
     for px in range(4):
         rs_gu[px] = gu_t[:, px * 128 : px * 128 + 128]
-    relay_gu, finish_gu = ring_sum("gu", rs_gu, in_gu, 256, 256, x, at_x)
 
     swap_att.wait_recv()
     swap["sg"].wait_recv()
@@ -471,22 +475,23 @@
             rs_h[i, 32 * px : 32 * px + 32, :] = inner[
                 80 * i + 48 : 80 * i + 80, px * 128 : px * 128 + 128
             ]
-    relay_g, finish_g = ring_sum("g", rs_g, in_g, 96, 96, x, at_x)
-    relay_h, finish_h = ring_sum("h", rs_h, in_h, 64, 64, y, at_y)
-
-    relay_gd()
-    relay_gu()
-    relay_g()
-    relay_h()
-
-    gd_1 = finish_gd()
+    finish_g = direct_sum("g", rs_g, in_g, x, at_x)
+    finish_h = direct_sum("h", rs_h, in_h, y, at_y)
+    finish_gu = direct_sum("gu", rs_gu, in_gu, x, at_x)
+
     h_1 = finish_h()
     for px in range(4):
-        rs_y2[px, 0:128, :] = gd_1[px * 128 : px * 128 + 128].astype(BF16)
-        rs_y2[px, 128:160, :] = h_1[px * 32 : px * 32 + 32].astype(BF16)
-    relay_y2, finish_y2 = ring_sum("y2", rs_y2, in_y2, 80, 80, x, at_x)
+        rs_h2[px] = h_1[px * 32 : px * 32 + 32].astype(BF16)
+    finish_h2 = direct_sum("h2", rs_h2, in_h2, x, at_x)
+    g_1 = finish_g()
+    for py in range(4):
+        rs_g2[py] = g_1[py * 48 : py * 48 + 48].astype(BF16)
+    finish_g2 = direct_sum("g2", rs_g2, in_g2, y, at_y)
+    gd_1 = finish_gd()
+    for px in range(4):
+        rs_gd2[px] = gd_1[px * 128 : px * 128 + 128].astype(BF16)
+    finish_gd2 = direct_sum("gd2", rs_gd2, in_gd2, x, at_x)
     gu_1 = finish_gu()
-    g_1 = finish_g()
     lane128 = iota((128, 128), 1)
     for py in range(4):
         first = gu_1[(py % 2) * 256 : (py % 2) * 256 + 128]
@@ -495,30 +500,30 @@
             pair = jnp.where(lane128 < 64, first, pltpu.roll(second, 64, 1))
         else:
             pair = jnp.where(lane128 < 64, pltpu.roll(first, 64, 1), second)
-        rs_x2[py, 0:128, :] = pair.astype(BF16)
-        rs_x2[py, 128:176, :] = g_1[py * 48 : py * 48 + 48].astype(BF16)
-    relay_x2, finish_x2 = ring_sum("x2", rs_x2, in_x2, 96, 80, y, at_y)
-    relay_y2()
-    relay_x2()
-    y_2 = finish_y2()
-    x_2 = finish_x2()
-
-    zg[0] = x_2[128:176].astype(BF16)
-    zg[1] = jnp.concatenate([x_2[160:176], y_2[128:160]], axis=0).astype(BF16)
-    holder = z // 2 == y
+        rs_gu2[py] = pair.astype(BF16)
+    finish_gu2 = direct_sum("gu2", rs_gu2, in_gu2, y, at_y)
+    h_2 = finish_h2()
+    g_2 = finish_g2()
+
+    zg[0] = g_2.astype(BF16)
+    zg[1] = jnp.concatenate([g_2[32:48], h_2], axis=0).astype(BF16)
     inner_copies = []
     for step in range(1, 8):
         to = (z + step) % 8
-        copy = describe("zg%d" % step, zg.at[to % 2], zgr.at[step - 1], at_z(step))
+        copy = describe(
+            zg.at[to % 2], zgr.at[step - 1], at_z(step), N_SEND + step - 1, "zg%d" % step
+        )
         goes = to // 2 == y
         pl.when(goes)(copy.start)
         inner_copies.append((copy, goes))
+    gd_2 = finish_gd2()
+    gu_2 = finish_gu2()
     lane32 = iota((32, 128), 1)
     for pz in range(8):
-        up = x_2[(pz % 4) * 32 : (pz % 4) * 32 + 32]
+        up = gu_2[(pz % 4) * 32 : (pz % 4) * 32 + 32]
         if pz // 4 == 1:
             up = pltpu.roll(up, 64, 1)
-        down = y_2[(pz // 2) * 32 : (pz // 2) * 32 + 32]
+        down = gd_2[(pz // 2) * 32 : (pz // 2) * 32 + 32]
         if pz % 2 == 0:
             down = pltpu.roll(down, 64, 1)
         zs[pz] = jnp.where(lane32 < 64, up, down).astype(BF16)
@@ -531,7 +536,8 @@
         for pc in range(2):
             for half in range(2):
                 target = device((x + step) % 4, pc, core + 2 * half, z)
-                copy = describe("ag%d%d%d" % (step, pc, half), ag, gr.at[x], target, "ag%d" % step)
+                slot = N_SEND + 7 + len(spread)
+                copy = describe(ag, gr.at[x], target, slot, "ag%d" % step)
                 goes = holder
                 if step == 0:
                     goes = holder & ((core != pc) | (y != core + 2 * half))
@@ -547,7 +553,6 @@
 
     for copy, goes in spread:
         pl.when(goes)(copy.start)
-    mine = holder & (core == y_lo)
 
     @pl.when(mine)
     def _():
@@ -568,7 +573,7 @@
     sums_ref[32:72, 0:80] = product
     for copy, goes in inner_copies + spread:
         pl.when(goes)(copy.wait_send)
-    for copy in started:
+    for copy in started[-N_SEND:]:
         copy.wait_send()
 
 
@@ -606,13 +611,13 @@
         low(SLOTS, DEC), low(SLOTS, FF), low(2, SLOTS, 256), low(2, SLOTS, DEC), low(SLOTS, DEC),
         low(SLOTS, DEC), low(SLOTS, FF), low(SLOTS, 256), low(SLOTS, DEC), low(SLOTS, DEC),
         low(4, 512, 128), low(4, 512, 128), low(4, 192, 128), low(4, 128, 128),
-        low(4, 176, 128), low(4, 160, 128),
-        low(4, 512, 128), low(4, 512, 128), low(4, 192, 128), low(4, 128, 128),
-        low(4, 176, 128), low(4, 160, 128),
+        low(4, 128, 128), low(4, 128, 128), low(4, 48, 128), low(4, 32, 128),
+        low(3, 512, 128), low(3, 512, 128), low(3, 192, 128), low(3, 128, 128),
+        low(3, 128, 128), low(3, 128, 128), low(3, 48, 128), low(3, 32, 128),
         low(8, 32, 128), low(7, 32, 128), low(2, 48, 128), low(7, 48, 128), low(48, 128),
         low(4, 48, 128),
-        pltpu.SemaphoreType.DMA((N_REMOTE,)),
-        pltpu.SemaphoreType.DMA((N_REMOTE,)),
+        pltpu.SemaphoreType.DMA((N_SEND + 7 + 16,)),
+        pltpu.SemaphoreType.DMA((N_RECV,)),
         pltpu.SemaphoreType.DMA((N_LOCAL,)),
     ]
     sums = pl.pallas_call(

time: 76 us -> 71.4 us (0.939)
  Pallas kernels: 75.2 us -> 70.6 us
    pallas_call x1, Pallas kernels: 73.8 us -> 69.2 us  [on_device(): pl.pallas_call(kernel, out_shape=jax.ShapeDtypeStruct((80, 128), F32), in...]
where the time goes in v3:
time: 71.4 us; the launch traced here: 71.3 us
  Pallas kernels  70.6 us (99%)
    pallas_call x1, Pallas kernels, on_device(): pl.pallas_call(kernel, out_shape=jax.ShapeDtypeStruct((80, 128), F32), in...  69.2 us
    pallas_call x1, Pallas kernels, on_device(): pl.pallas_call(split_sums, out_shape=(jax.ShapeDtypeStruct((40, 80), F32)...  1.46 us

profile of v3, /device:TPU:1, one launch (start us, length us, event | category | flops | bytes accessed | tf_op | source)
XLA Modules:
  0.0 71.3 jit_solution(5446666710408168090)
XLA Ops:
  0.6 69.2 %shard_map.130.sums_ref = f32[80,128]{1,0:T(8,128)} custom-call(bf16[384,1280]{1,0:T(8,128)(2,1)} %bitcast.7, bf16[1176,384]{1,0:T(8,128)(2,1)} %bitcast.8, s32[1,384]{1,0:T(1,128)} %vis_ref.1, bf16[1280,1920]{1,0:T(8,128)(2,1)} %wqkv_h.1, bf16[640,1280]{1,0:T(8,128)(2,1)} %wout_h.1, bf16[1280,512]{1,0:T(8,128)(2,1)} %wembed_h.1, bf16[512]{0:T(512)(128)(2,1)} %mtok_ref.1, ...), custom_call_target="tpu_custom_call" | custom-call | tf_op jit(solution)/shard_map/pallas_call | solution.py:623
  69.8 1.5 %shard_map.131 = (f32[40,80]{1,0:T(8,128)}, f32[32,64]{1,0:T(8,128)}, f32[32,64]{1,0:T(8,128)}) custom-call(f32[80,128]{1,0:T(8,128)} %shard_map.130.sums_ref), custom_call_target="tpu_custom_call" | custom-call | tf_op jit(solution)/shard_map/pallas_call | solution.py:639

commit v4 on v3

--- a/solution.py
+++ b/solution.py
@@ -62,7 +62,7 @@
 
 
 N_SEND = 32
-N_RECV = 88
+N_NAMED = 75
 N_LOCAL = 14
 
 
@@ -74,8 +74,8 @@
     att_out, att_in, att, att_sib, pos_slot, tgt_slot, mask_slot,
     unit_m, act_m, og_m, hg_m, unit_ms, act_ms, og_ms, hg_ms, gd_acc, gu_acc,
     unit_v, act_v, og_v, hg_v, sg_v, unit_vs, act_vs, og_vs, hg_vs, sg_vs,
-    rs_gd, rs_gu, rs_g, rs_h, rs_gd2, rs_gu2, rs_g2, rs_h2,
-    in_gd, in_gu, in_g, in_h, in_gd2, in_gu2, in_g2, in_h2,
+    rs_gd, rs_gu, rs_g, rs_gd2, rs_gu2,
+    in_gd, in_gu, in_g, in_gd2, in_gu2,
     zs, zr, zg, zgr, ag, gr,
     send_sem, recv_sem, load_sem,
 ):
@@ -114,23 +114,23 @@
             load(name + str(part), wqkv_h.at[span, pl.ds(first, 640)], dst.at[span])
 
     barrier = pltpu.get_barrier_semaphore()
-    holder = z // 2 == y
-    mine = holder & (core == y_lo)
+    user = core == y_lo
     peers = [sibling] + [at_z(step) for step in range(1, 8)]
     peers += [at_x(step) for step in range(1, 4)] + [at_y(step) for step in range(1, 4)]
     for peer in peers:
         pl.semaphore_signal(barrier, inc=1, device_id=peer, device_id_type=MESH)
-    for step in range(4):
-        source = device((x + step) % 4, y_lo, z // 2, z)
-
-        def greet():
-            pl.semaphore_signal(barrier, inc=1, device_id=source, device_id_type=MESH)
-
-        if step == 0:
-            pl.when(jnp.logical_not(mine))(greet)
-        else:
-            greet()
-    greetings = len(peers) + jnp.where(holder, 16, 0) - jnp.where(mine, 1, 0)
+    for px in range(4):
+        for py in range(4):
+            source = device((x + px) % 4, y_lo, (y + py) % 4, z)
+
+            def greet():
+                pl.semaphore_signal(barrier, inc=1, device_id=source, device_id_type=MESH)
+
+            if px or py:
+                greet()
+            else:
+                pl.when(jnp.logical_not(user))(greet)
+    greetings = len(peers) + 16 - jnp.where(user, 1, 0)
 
     started = []
 
@@ -139,7 +139,7 @@
             src_ref=src,
             dst_ref=dst,
             send_sem=send_sem.at[slot],
-            recv_sem=recv_sem.at[ident(name)],
+            recv_sem=recv_sem.at[ident(name) if isinstance(name, str) else name],
             device_id=target,
             device_id_type=MESH,
         )
@@ -469,24 +469,19 @@
     swap["sg"].wait_recv()
     inner = dot_tn(att[core], sg_v[...]) + dot_tn(att_sib[...], sg_vs[...])
     inner = inner.astype(BF16)
-    for px in range(4):
-        for i in range(4):
-            rs_g[px, 48 * i : 48 * i + 48, :] = inner[80 * i : 80 * i + 48, px * 128 : px * 128 + 128]
-            rs_h[i, 32 * px : 32 * px + 32, :] = inner[
-                80 * i + 48 : 80 * i + 80, px * 128 : px * 128 + 128
-            ]
-    finish_g = direct_sum("g", rs_g, in_g, x, at_x)
-    finish_h = direct_sum("h", rs_h, in_h, y, at_y)
+    for py in range(4):
+        rs_g[py] = inner[:, py * 128 : py * 128 + 128]
+    finish_g = direct_sum("g", rs_g, in_g, y, at_y)
     finish_gu = direct_sum("gu", rs_gu, in_gu, x, at_x)
 
-    h_1 = finish_h()
-    for px in range(4):
-        rs_h2[px] = h_1[px * 32 : px * 32 + 32].astype(BF16)
-    finish_h2 = direct_sum("h2", rs_h2, in_h2, x, at_x)
     g_1 = finish_g()
-    for py in range(4):
-        rs_g2[py] = g_1[py * 48 : py * 48 + 48].astype(BF16)
-    finish_g2 = direct_sum("g2", rs_g2, in_g2, y, at_y)
+    for pz in range(8):
+        piece = jnp.concatenate([g_1[40 * pz : 40 * pz + 40], jnp.zeros((8, 128), F32)], axis=0)
+        zg[pz] = piece.astype(BF16)
+    row_copies = [
+        send("zg%d" % step, zg.at[(z + step) % 8], zgr.at[step - 1], at_z(step))
+        for step in range(1, 8)
+    ]
     gd_1 = finish_gd()
     for px in range(4):
         rs_gd2[px] = gd_1[px * 128 : px * 128 + 128].astype(BF16)
@@ -502,20 +497,31 @@
             pair = jnp.where(lane128 < 64, pltpu.roll(first, 64, 1), second)
         rs_gu2[py] = pair.astype(BF16)
     finish_gu2 = direct_sum("gu2", rs_gu2, in_gu2, y, at_y)
-    h_2 = finish_h2()
-    g_2 = finish_g2()
-
-    zg[0] = g_2.astype(BF16)
-    zg[1] = jnp.concatenate([g_2[32:48], h_2], axis=0).astype(BF16)
-    inner_copies = []
+    total = zg[z].astype(F32)
     for step in range(1, 8):
-        to = (z + step) % 8
-        copy = describe(
-            zg.at[to % 2], zgr.at[step - 1], at_z(step), N_SEND + step - 1, "zg%d" % step
-        )
-        goes = to // 2 == y
-        pl.when(goes)(copy.start)
-        inner_copies.append((copy, goes))
+        row_copies[step - 1].wait_recv()
+        total = total + zgr[step - 1].astype(F32)
+    ag[...] = total.astype(BF16)
+    spread = []
+    for px in range(4):
+        for pc in range(2):
+            for half in range(2):
+                target = device((x + px) % 4, pc, core + 2 * half, z)
+                away = None
+                if px == 0:
+                    away = (core != pc) | (y != core + 2 * half)
+                slot = N_SEND + len(spread)
+                copy = describe(ag, gr.at[y, x], target, slot, N_NAMED + y * 4 + x)
+                if away is None:
+                    copy.start()
+                else:
+                    pl.when(away)(copy.start)
+                spread.append((copy, away))
+
+    @pl.when(user)
+    def _():
+        gr[y, x] = ag[...]
+
     gd_2 = finish_gd2()
     gu_2 = finish_gu2()
     lane32 = iota((32, 128), 1)
@@ -531,48 +537,30 @@
     for step in range(1, 8):
         last.append(send("z%d" % step, zs.at[(z + step) % 8], zr.at[step - 1], at_z(step)))
 
-    spread = []
-    for step in range(4):
-        for pc in range(2):
-            for half in range(2):
-                target = device((x + step) % 4, pc, core + 2 * half, z)
-                slot = N_SEND + 7 + len(spread)
-                copy = describe(ag, gr.at[x], target, slot, "ag%d" % step)
-                goes = holder
-                if step == 0:
-                    goes = holder & ((core != pc) | (y != core + 2 * half))
-                spread.append((copy, goes))
-
-    @pl.when(holder)
-    def _():
-        total = zg[z % 2].astype(F32)
-        for step in range(1, 8):
-            inner_copies[step - 1][0].wait_recv()
-            total = total + zgr[step - 1].astype(F32)
-        ag[...] = total.astype(BF16)
-
-    for copy, goes in spread:
-        pl.when(goes)(copy.start)
-
-    @pl.when(mine)
-    def _():
-        gr[x] = ag[...]
-
     result = zs[z].astype(F32)
     for step in range(1, 8):
         last[step - 1].wait_recv()
         result = result + zr[step - 1].astype(F32)
     sums_ref[0:32, :] = result
-    pl.when(jnp.logical_not(mine))(spread[0][0].wait_recv)
-    for step in range(1, 4):
-        spread[step * 4][0].wait_recv()
-    rows_b = jnp.concatenate([gr[i] for i in range(4)], axis=1)
+    for py in range(4):
+        for px in range(4):
+            landed = describe(ag, gr.at[py, px], sibling, 0, N_NAMED + py * 4 + px)
+            here = user & (y == py) & (x == px)
+            pl.when(jnp.logical_not(here))(landed.wait_recv)
+    rows_b = []
+    for py in range(4):
+        total = gr[py, 0].astype(F32)
+        for px in range(1, 4):
+            total = total + gr[py, px].astype(F32)
+        rows_b.append(total.astype(BF16))
+    rows_b = jnp.concatenate(rows_b, axis=1)
     columns = pl.ds(pl.multiple_of((x * 4 + core * 2 + seg) * 80, 16), 80)
-    product = dot_nt(rows_b, wembed[columns, :])
-    product = jnp.where(z % 2 == 0, product[0:40], product[8:48])
-    sums_ref[32:72, 0:80] = product
-    for copy, goes in inner_copies + spread:
-        pl.when(goes)(copy.wait_send)
+    sums_ref[32:72, 0:80] = dot_nt(rows_b, wembed[columns, :])[0:40]
+    for copy, away in spread:
+        if away is None:
+            copy.wait_send()
+        else:
+            pl.when(away)(copy.wait_send)
     for copy in started[-N_SEND:]:
         copy.wait_send()
 
@@ -610,14 +598,12 @@
         wide(256, FF), wide(DEC, DEC),
         low(SLOTS, DEC), low(SLOTS, FF), low(2, SLOTS, 256), low(2, SLOTS, DEC), low(SLOTS, DEC),
         low(SLOTS, DEC), low(SLOTS, FF), low(SLOTS, 256), low(SLOTS, DEC), low(SLOTS, DEC),
-        low(4, 512, 128), low(4, 512, 128), low(4, 192, 128), low(4, 128, 128),
-        low(4, 128, 128), low(4, 128, 128), low(4, 48, 128), low(4, 32, 128),
-        low(3, 512, 128), low(3, 512, 128), low(3, 192, 128), low(3, 128, 128),
-        low(3, 128, 128), low(3, 128, 128), low(3, 48, 128), low(3, 32, 128),
-        low(8, 32, 128), low(7, 32, 128), low(2, 48, 128), low(7, 48, 128), low(48, 128),
-        low(4, 48, 128),
-        pltpu.SemaphoreType.DMA((N_SEND + 7 + 16,)),
-        pltpu.SemaphoreType.DMA((N_RECV,)),
+        low(4, 512, 128), low(4, 512, 128), low(4, 320, 128), low(4, 128, 128), low(4, 128, 128),
+        low(3, 512, 128), low(3, 512, 128), low(3, 320, 128), low(3, 128, 128), low(3, 128, 128),
+        low(8, 32, 128), low(7, 32, 128), low(8, 48, 128), low(7, 48, 128), low(48, 128),
+        low(4, 4, 48, 128),
+        pltpu.SemaphoreType.DMA((N_SEND + 16,)),
+        pltpu.SemaphoreType.DMA((N_NAMED + 16,)),
         pltpu.SemaphoreType.DMA((N_LOCAL,)),
     ]
     sums = pl.pallas_call(

time: 71.4 us -> 71.4 us (level)
  no operation moved by 1% of the time
where the time goes in v4:
time: 71.4 us; the launch traced here: 71.2 us
  Pallas kernels  70.6 us (99%)
    pallas_call x1, Pallas kernels, on_device(): pl.pallas_call(kernel, out_shape=jax.ShapeDtypeStruct((80, 128), F32), in...  69.1 us
    pallas_call x1, Pallas kernels, on_device(): pl.pallas_call(split_sums, out_shape=(jax.ShapeDtypeStruct((40, 80), F32)...  1.46 us

profile of v4, /device:TPU:1, one launch (start us, length us, event | category | flops | bytes accessed | tf_op | source)
XLA Modules:
  0.0 71.2 jit_solution(8612651727310479770)
XLA Ops:
  0.6 69.1 %shard_map.130.sums_ref = f32[80,128]{1,0:T(8,128)} custom-call(bf16[384,1280]{1,0:T(8,128)(2,1)} %bitcast.7, bf16[1176,384]{1,0:T(8,128)(2,1)} %bitcast.8, s32[1,384]{1,0:T(1,128)} %vis_ref.1, bf16[1280,1920]{1,0:T(8,128)(2,1)} %wqkv_h.1, bf16[640,1280]{1,0:T(8,128)(2,1)} %wout_h.1, bf16[1280,512]{1,0:T(8,128)(2,1)} %wembed_h.1, bf16[512]{0:T(512)(128)(2,1)} %mtok_ref.1, ...), custom_call_target="tpu_custom_call" | custom-call | tf_op jit(solution)/shard_map/pallas_call | solution.py:609
  69.8 1.5 %shard_map.131 = (f32[40,80]{1,0:T(8,128)}, f32[32,64]{1,0:T(8,128)}, f32[32,64]{1,0:T(8,128)}) custom-call(f32[80,128]{1,0:T(8,128)} %shard_map.130.sums_ref), custom_call_target="tpu_custom_call" | custom-call | tf_op jit(solution)/shard_map/pallas_call | solution.py:625

commit v5 on v4

--- a/solution.py
+++ b/solution.py
@@ -61,21 +61,21 @@
     return names.index(name)
 
 
-N_SEND = 32
-N_NAMED = 75
-N_LOCAL = 14
+N_SEND = 16
+N_NAMED = 78
+N_LOCAL = 11
 
 
 def kernel(
     tokens_h, targets_h, vis_ref, wqkv_h, wout_h, wembed_h, mtok_ref, dpos_h, wup_h, wdown_h, whead_h,
     sums_ref,
     tokens, targets, wq, wk, wv, wout, wembed, dpos, wup, wdown, whead,
-    selector, seen_col, packed, heads, other, kv_own, kv_r, kv_l, keys, vals, qx, acc, top,
+    selector, seen_col, packed, heads, other, kv_own, kv_r, kv_l, kv_d, keys, vals, qx, acc, top,
     att_out, att_in, att, att_sib, pos_slot, tgt_slot, mask_slot,
     unit_m, act_m, og_m, hg_m, unit_ms, act_ms, og_ms, hg_ms, gd_acc, gu_acc,
     unit_v, act_v, og_v, hg_v, sg_v, unit_vs, act_vs, og_vs, hg_vs, sg_vs,
-    rs_gd, rs_gu, rs_g, rs_gd2, rs_gu2,
-    in_gd, in_gu, in_g, in_gd2, in_gu2,
+    rs_gd, rs_gu, rs_g, rs_h, rs_gd2, rs_gu2,
+    in_gd, in_gu, in_g, in_h, in_gd2, in_gu2,
     zs, zr, zg, zgr, ag, gr,
     send_sem, recv_sem, load_sem,
 ):
@@ -109,9 +109,7 @@
 
     load("tokens", tokens_h, tokens)
     for name, dst, first in (("wk", wk, 640), ("wv", wv, 1280), ("wq", wq, 0)):
-        for part in range(2):
-            span = pl.ds(part * 640, 640)
-            load(name + str(part), wqkv_h.at[span, pl.ds(first, 640)], dst.at[span])
+        load(name, wqkv_h.at[:, pl.ds(first, 640)], dst)
 
     barrier = pltpu.get_barrier_semaphore()
     user = core == y_lo
@@ -168,16 +166,8 @@
     seen_col[...] = dot_tn(chosen, jnp.ones((ROWS, 128), BF16))
     projected = []
     for name, weight in (("wk", wk), ("wv", wv), ("wq", wq)):
-        loads[name + "0"].wait()
-        loads[name + "1"].wait()
+        loads[name].wait()
         projected.append(dot(normed, weight[...]))
-    load("dpos", dpos_h, dpos)
-    load("targets", targets_h, targets)
-    load("wup", wup_h, wup)
-    load("wdown", wdown_h, wdown)
-    load("whead", whead_h, whead)
-    load("wout", wout_h, wout)
-    load("wembed", wembed_h, wembed)
     slot_row = iota((ROWS, 256), 0)
     for h in range(HEADS):
         parts = [p[:, h * 80 : h * 80 + 80] for p in projected]
@@ -240,7 +230,7 @@
         ring[way, part, step, half] = send(
             "%s%d%d%d" % (way, step, part, half),
             src.at[rows_of],
-            buffer.at[part, step, rows_of],
+            (buffer if step < 3 else kv_d).at[part, step % 3, rows_of],
             at_z(to),
         )
 
@@ -253,12 +243,19 @@
         for half in range(2):
             for way, buffer in (("r", kv_r), ("l", kv_l)):
                 ring[way, part, step, half].wait_recv()
-                if step < 2 or (step == 2 and (way == "r") == (part == 0)):
+                if step < 2 or (way == "r") == (half == 0):
                     ring_send(way, part, step + 1, half, buffer.at[part, step])
 
     own = [heads[y * 2], heads[y * 2 + 1]]
     fold(own[0], own[1], kv_own.at[0])
     ring_start(0)
+    load("dpos", dpos_h, dpos)
+    load("targets", targets_h, targets)
+    load("wup", wup_h, wup)
+    load("wdown", wdown_h, wdown)
+    load("whead", whead_h, whead)
+    load("wout", wout_h, wout)
+    load("wembed", wembed_h, wembed)
     for j in range(2):
         make_query(own[j], j, 0)
     from_down.wait_recv()
@@ -377,11 +374,11 @@
     attend(12 * ROWS, kv_r.at[1, 2], kv_l.at[1, 2])
     loads["wout"].wait()
     loads["wembed"].wait()
-    for half in range(2):
-        ring["r", 0, 3, half].wait_recv()
-        ring["l", 1, 3, half].wait_recv()
-    unfold(kv_r.at[0, 3], 14 * ROWS)
-    unfold(kv_l.at[1, 3], 15 * ROWS)
+    for part in range(2):
+        ring["r", part, 3, 0].wait_recv()
+        ring["l", part, 3, 1].wait_recv()
+    unfold(kv_d.at[0, 0], 14 * ROWS)
+    unfold(kv_d.at[1, 0], 15 * ROWS)
 
     back = []
     for j in range(2):
@@ -464,19 +461,22 @@
     gu_t = gu_t.astype(BF16)
     for px in range(4):
         rs_gu[px] = gu_t[:, px * 128 : px * 128 + 128]
+    finish_gu = direct_sum("gu", rs_gu, in_gu, x, at_x)
 
     swap_att.wait_recv()
     swap["sg"].wait_recv()
     inner = dot_tn(att[core], sg_v[...]) + dot_tn(att_sib[...], sg_vs[...])
     inner = inner.astype(BF16)
-    for py in range(4):
-        rs_g[py] = inner[:, py * 128 : py * 128 + 128]
-    finish_g = direct_sum("g", rs_g, in_g, y, at_y)
-    finish_gu = direct_sum("gu", rs_gu, in_gu, x, at_x)
-
-    g_1 = finish_g()
+    for p in range(4):
+        rs_g[p] = inner[0:160, p * 128 : p * 128 + 128]
+        rs_h[p] = inner[160:320, p * 128 : p * 128 + 128]
+    finish_g = direct_sum("g", rs_g, in_g, x, at_x)
+    finish_h = direct_sum("h", rs_h, in_h, y, at_y)
+
+    g_1 = (finish_g(), finish_h())
     for pz in range(8):
-        piece = jnp.concatenate([g_1[40 * pz : 40 * pz + 40], jnp.zeros((8, 128), F32)], axis=0)
+        r = 40 * (pz % 4)
+        piece = jnp.concatenate([g_1[pz // 4][r : r + 40], jnp.zeros((8, 128), F32)], axis=0)
         zg[pz] = piece.astype(BF16)
     row_copies = [
         send("zg%d" % step, zg.at[(z + step) % 8], zgr.at[step - 1], at_z(step))
@@ -547,13 +547,10 @@
             landed = describe(ag, gr.at[py, px], sibling, 0, N_NAMED + py * 4 + px)
             here = user & (y == py) & (x == px)
             pl.when(jnp.logical_not(here))(landed.wait_recv)
-    rows_b = []
-    for py in range(4):
-        total = gr[py, 0].astype(F32)
-        for px in range(1, 4):
-            total = total + gr[py, px].astype(F32)
-        rows_b.append(total.astype(BF16))
-    rows_b = jnp.concatenate(rows_b, axis=1)
+    blocks = [[gr[py, px].astype(F32) for px in range(4)] for py in range(4)]
+    by_x = jnp.concatenate([sum(blocks[py][p] for py in range(4)) for p in range(4)], axis=1)
+    by_y = jnp.concatenate([sum(blocks[p][px] for px in range(4)) for p in range(4)], axis=1)
+    rows_b = jnp.where(z < 4, by_x, by_y).astype(BF16)
     columns = pl.ds(pl.multiple_of((x * 4 + core * 2 + seg) * 80, 16), 80)
     sums_ref[32:72, 0:80] = dot_nt(rows_b, wembed[columns, :])[0:40]
     for copy, away in spread:
@@ -588,7 +585,7 @@
         low(TILE, D), low(PIX, TILE), low(D, INNER), low(D, INNER), low(D, INNER), low(INNER, D),
         low(D, DEC), low(TILE, DEC), low(DEC, FF), low(FF, DEC), low(PIX, DEC),
         low(ROWS, TILE), wide(TILE, 128), low(ROWS, D), low(HEADS, ROWS, 256), low(2, ROWS, 256),
-        low(2, PART, 128), low(2, 4, PART, 128), low(2, 4, PART, 128),
+        low(2, PART, 128), low(2, 3, PART, 128), low(2, 3, PART, 128), low(2, 1, PART, 128),
         low(2, 16 * ROWS, 128), low(2, 16 * ROWS, 128), low(2, 2 * ROWS, 128),
         wide(2, 2 * ROWS, 128), wide(2, 2 * ROWS, 128),
         low(2, 2, ROWS, 128), low(4, 2, SLOTS, 128), low(2, SLOTS, 320), low(SLOTS, 320),
@@ -598,8 +595,8 @@
         wide(256, FF), wide(DEC, DEC),
         low(SLOTS, DEC), low(SLOTS, FF), low(2, SLOTS, 256), low(2, SLOTS, DEC), low(SLOTS, DEC),
         low(SLOTS, DEC), low(SLOTS, FF), low(SLOTS, 256), low(SLOTS, DEC), low(SLOTS, DEC),
-        low(4, 512, 128), low(4, 512, 128), low(4, 320, 128), low(4, 128, 128), low(4, 128, 128),
-        low(3, 512, 128), low(3, 512, 128), low(3, 320, 128), low(3, 128, 128), low(3, 128, 128),
+        low(4, 512, 128), low(4, 512, 128), low(4, 160, 128), low(4, 160, 128), low(4, 128, 128), low(4, 128, 128),
+        low(3, 512, 128), low(3, 512, 128), low(3, 160, 128), low(3, 160, 128), low(3, 128, 128), low(3, 128, 128),
         low(8, 32, 128), low(7, 32, 128), low(8, 48, 128), low(7, 48, 128), low(48, 128),
         low(4, 4, 48, 128),
         pltpu.SemaphoreType.DMA((N_SEND + 16,)),

time: 71.4 us -> 70.7 us (level)
  Pallas kernels: 70.6 us -> 69.8 us
    pallas_call x1, Pallas kernels: 69.1 us -> 68.4 us  [on_device(): pl.pallas_call(kernel, out_shape=jax.ShapeDtypeStruct((80, 128), F32), in...]
where the time goes in v5:
time: 70.7 us; the launch traced here: 70.5 us
  Pallas kernels  69.8 us (99%)
    pallas_call x1, Pallas kernels, on_device(): pl.pallas_call(kernel, out_shape=jax.ShapeDtypeStruct((80, 128), F32), in...  68.4 us
    pallas_call x1, Pallas kernels, on_device(): pl.pallas_call(split_sums, out_shape=(jax.ShapeDtypeStruct((40, 80), F32)...  1.46 us

profile of v5, /device:TPU:1, one launch (start us, length us, event | category | flops | bytes accessed | tf_op | source)
XLA Modules:
  0.0 70.5 jit_solution(14857517114080898299)
XLA Ops:
  0.6 68.4 %shard_map.130.sums_ref = f32[80,128]{1,0:T(8,128)} custom-call(bf16[384,1280]{1,0:T(8,128)(2,1)} %bitcast.7, bf16[1176,384]{1,0:T(8,128)(2,1)} %bitcast.8, s32[1,384]{1,0:T(1,128)} %vis_ref.1, bf16[1280,1920]{1,0:T(8,128)(2,1)} %wqkv_h.1, bf16[640,1280]{1,0:T(8,128)(2,1)} %wout_h.1, bf16[1280,512]{1,0:T(8,128)(2,1)} %wembed_h.1, bf16[512]{0:T(512)(128)(2,1)} %mtok_ref.1, ...), custom_call_target="tpu_custom_call" | custom-call | tf_op jit(solution)/shard_map/pallas_call | solution.py:606
  69.0 1.5 %shard_map.131 = (f32[40,80]{1,0:T(8,128)}, f32[32,64]{1,0:T(8,128)}, f32[32,64]{1,0:T(8,128)}) custom-call(f32[80,128]{1,0:T(8,128)} %shard_map.130.sums_ref), custom_call_target="tpu_custom_call" | custom-call | tf_op jit(solution)/shard_map/pallas_call | solution.py:622

commit v6 on v5

--- a/solution.py
+++ b/solution.py
@@ -63,11 +63,11 @@
 
 N_SEND = 16
 N_NAMED = 78
-N_LOCAL = 11
+N_LOCAL = 13
 
 
 def kernel(
-    tokens_h, targets_h, vis_ref, wqkv_h, wout_h, wembed_h, mtok_ref, dpos_h, wup_h, wdown_h, whead_h,
+    tokens_h, targets_h, vis_h, wqkv_h, wout_h, wembed_h, mtok_h, dpos_h, wup_h, wdown_h, whead_h,
     sums_ref,
     tokens, targets, wq, wk, wv, wout, wembed, dpos, wup, wdown, whead,
     selector, seen_col, packed, heads, other, kv_own, kv_r, kv_l, kv_d, keys, vals, qx, acc, top,
@@ -77,7 +77,7 @@
     rs_gd, rs_gu, rs_g, rs_h, rs_gd2, rs_gu2,
     in_gd, in_gu, in_g, in_h, in_gd2, in_gu2,
     zs, zr, zg, zgr, ag, gr,
-    send_sem, recv_sem, load_sem,
+    vis_ref, mtok_ref, send_sem, recv_sem, load_sem,
 ):
     dp = lax.axis_index("dp")
     seg = lax.axis_index("segment")
@@ -107,6 +107,7 @@
         copy.start()
         loads[name] = copy
 
+    load("vis", vis_h, vis_ref)
     load("tokens", tokens_h, tokens)
     for name, dst, first in (("wk", wk, 640), ("wv", wv, 1280), ("wq", wq, 0)):
         load(name, wqkv_h.at[:, pl.ds(first, 640)], dst)
@@ -151,6 +152,7 @@
         started.append(copy)
         return copy
 
+    loads["vis"].wait()
     vis = vis_ref[...].astype(F32)
     tri = (iota((TILE, TILE), 0) <= iota((TILE, TILE), 1)).astype(F32).astype(BF16)
     vis8 = jnp.broadcast_to(vis, (8, TILE))
@@ -249,6 +251,7 @@
     own = [heads[y * 2], heads[y * 2 + 1]]
     fold(own[0], own[1], kv_own.at[0])
     ring_start(0)
+    load("mtok", mtok_h, mtok_ref)
     load("dpos", dpos_h, dpos)
     load("targets", targets_h, targets)
     load("wup", wup_h, wup)
@@ -326,7 +329,7 @@
         og[1] = mixed[:, 256:512]
 
     attend(0, kv_own.at[0], kv_own.at[1], begin=True)
-    for name in ("dpos", "targets", "wup", "wdown", "whead"):
+    for name in ("mtok", "dpos", "targets", "wup", "wdown", "whead"):
         loads[name].wait()
     ring_next(0, 0)
     part_rows = pl.ds(pl.multiple_of(seg * HALF, 16), HALF)
@@ -599,6 +602,7 @@
         low(3, 512, 128), low(3, 512, 128), low(3, 160, 128), low(3, 160, 128), low(3, 128, 128), low(3, 128, 128),
         low(8, 32, 128), low(7, 32, 128), low(8, 48, 128), low(7, 48, 128), low(48, 128),
         low(4, 4, 48, 128),
+        pltpu.VMEM((1, TILE), jnp.int32), low(DEC),
         pltpu.SemaphoreType.DMA((N_SEND + 16,)),
         pltpu.SemaphoreType.DMA((N_NAMED + 16,)),
         pltpu.SemaphoreType.DMA((N_LOCAL,)),
@@ -607,7 +611,7 @@
         kernel,
         out_shape=jax.ShapeDtypeStruct((80, 128), F32),
         in_specs=[
-            anywhere, anywhere, vmem, anywhere, anywhere, anywhere, vmem, anywhere, anywhere,
+            anywhere, anywhere, anywhere, anywhere, anywhere, anywhere, anywhere, anywhere, anywhere,
             anywhere, anywhere,
         ],
         out_specs=vmem,

time: 70.7 us -> 70.1 us (level)
  no operation moved by 1% of the time
where the time goes in v6:
time: 70.1 us; the launch traced here: 70 us
  Pallas kernels  69.4 us (99%)
    pallas_call x1, Pallas kernels, on_device(): pl.pallas_call(kernel, out_shape=jax.ShapeDtypeStruct((80, 128), F32), in...  67.9 us
    pallas_call x1, Pallas kernels, on_device(): pl.pallas_call(split_sums, out_shape=(jax.ShapeDtypeStruct((40, 80), F32)...  1.46 us

profile of v6, /device:TPU:1, one launch (start us, length us, event | category | flops | bytes accessed | tf_op | source)
XLA Modules:
  0.0 70.0 jit_solution(14059045971464562824)
XLA Ops:
  0.6 67.9 %shard_map.130.sums_ref = f32[80,128]{1,0:T(8,128)} custom-call(bf16[384,1280]{1,0:T(8,128)(2,1)} %bitcast.7, bf16[1176,384]{1,0:T(8,128)(2,1)} %bitcast.8, s32[1,384]{1,0:T(1,128)} %vis_h.1, bf16[1280,1920]{1,0:T(8,128)(2,1)} %wqkv_h.1, bf16[640,1280]{1,0:T(8,128)(2,1)} %wout_h.1, bf16[1280,512]{1,0:T(8,128)(2,1)} %wembed_h.1, bf16[512]{0:T(512)(128)(2,1)} %mtok_h.1, ...), custom_call_target="tpu_custom_call" | custom-call | tf_op jit(solution)/shard_map/pallas_call | solution.py:610
  68.6 1.5 %shard_map.131 = (f32[40,80]{1,0:T(8,128)}, f32[32,64]{1,0:T(8,128)}, f32[32,64]{1,0:T(8,128)}) custom-call(f32[80,128]{1,0:T(8,128)} %shard_map.130.sums_ref), custom_call_target="tpu_custom_call" | custom-call | tf_op jit(solution)/shard_map/pallas_call | solution.py:626
